TPU v7x, 256 devices: a whole 4x4x8 slice. The times are simulated.
256 devices in a mesh: segment: 2 (over core), latent: 16 (over y, x), dp: 8 (over z).
Axes of the slice: x: 4, y: 4, z: 8, core: 2. Of those that a mesh axis runs over, the one named last changes fastest.
Arguments:
- resid_in: bfloat16 [4, 128, 3584], P(None, 'dp', 'latent'), may hold values from -40 to 40
- norm_gain: float32 [2, 3584], P('segment'), may hold values from 0.25 to 1.75
- enc_weight: bfloat16 [2, 3584, 65536], P('segment', None, ('latent', 'dp')), may hold values from -0.09375 to 0.09375
- enc_bias: float32 [2, 65536], P('segment', ('latent', 'dp')), may hold values from -3 to 3
- dec_self: bfloat16 [2, 65536, 3584], P('segment', ('latent', 'dp')), may hold values from -0.25 to 0.25
- dec_cross: bfloat16 [65536, 3584], P(('latent', 'dp')), may hold values from -0.25 to 0.25
- block_ids: int32 [2, 4, 2, 128, 4], P('segment', None, None, ('latent', 'dp')), may hold values from 0 to 7, as said below
- block_counts: int32 [2, 4, 2, 128], P('segment', None, None, ('latent', 'dp')), may hold values from 1 to 4, as said below
Outputs:
- recon: bfloat16 [2, 4, 128, 3584], P('segment', None, 'dp', 'latent')
Inputs may be any that keep to these rules, and one draw needn't show every extreme that they name: `block_ids`: the 4 entries of one list are distinct local block numbers. `block_counts`: in every tile of every layer and micro-batch some device group has 4 live blocks.
All inputs are finite; a program needn't handle non-finite values.
Results may differ from a plain program's by a relative error of at most 0.007.
Values may be sent and summed in bfloat16 or wider, within the bound.
No kernel may reach another device: no remote copies, remote signals or barrier semaphores. Data moves between devices by JAX's collectives and lax.ppermute only.
A program may use at most 64 MiB of HBM per device.

v0:
```python
import jax
import jax.numpy as jnp
from jax import lax
from jax.sharding import PartitionSpec as P

BLK_DEV = 8
BLOCK = 64


norm_eps = 1e-06


def passed_along(value, axis, steps):
    count = lax.axis_size(axis)
    initial, last = (max(0, -steps), min(count, count - steps))
    return lax.ppermute(value, axis, [(source, source + steps) for source in range(initial, last)])


def normalize(resid, gain_row):
    values = resid.astype(jnp.float32)
    scaling = lax.rsqrt(jnp.mean(values * values, axis=-1, keepdims=True) + norm_eps)
    return (values * scaling * gain_row).astype(jnp.bfloat16)


def encode_every(normed, encoder, biases, list_ids, slot_live):
    tile_count = list_ids.shape[0]
    matches = (list_ids[..., None] == jnp.arange(BLK_DEV, dtype=jnp.int32)) & slot_live[..., None]
    live = jnp.any(matches, axis=1).astype(jnp.float32)
    before = jnp.dot(normed, encoder, preferred_element_type=jnp.float32) + biases
    before = before.reshape(tile_count, -1, BLK_DEV, BLOCK)
    active = jnp.maximum(before, 0.0) * live[:, None, :, None]
    return active.reshape(normed.shape[0], BLK_DEV * BLOCK).astype(jnp.bfloat16)


def reduce_owners(term_rows, own_rows):
    row_part = lax.psum_scatter(
        term_rows(jnp.int32(0), own_rows * lax.axis_size("dp")),
        "dp",
        scatter_dimension=0,
        tiled=True,
    )
    return lax.psum_scatter(row_part, "latent", scatter_dimension=1, tiled=True)


def body(resid_in, norm_gain, enc_weight, enc_bias, dec_self, dec_cross, block_ids, block_counts):
    segment_index = lax.axis_index("segment")
    is_first = segment_index == 0
    batch_count = resid_in.shape[0]
    own_rows = resid_in.shape[1]
    encoder = enc_weight[0]
    biases = enc_bias[0]
    decoder = dec_self[0]
    gain_row = norm_gain[0]
    list_all = block_ids[0, :, :, 0, :]
    count_all = block_counts[0, :, :, 0]
    held_resid = jnp.zeros_like(resid_in[0])
    carried = jnp.zeros(resid_in[0].shape, jnp.float32)
    outputs = []
    for step_index in range(batch_count + 1):
        fresh_input = resid_in[min(step_index, batch_count - 1)]
        current = jnp.where(is_first, fresh_input, held_resid)
        batch_pick = jnp.clip(step_index - segment_index, 0, batch_count - 1)
        list_ids = lax.dynamic_index_in_dim(list_all, batch_pick, 0, keepdims=False)
        list_counts = lax.dynamic_index_in_dim(count_all, batch_pick, 0, keepdims=False)
        slot_live = jnp.arange(list_ids.shape[1], dtype=jnp.int32)[None, :] < list_counts[:, None]
        whole_rows = lax.all_gather(current, "latent", axis=1, tiled=True)
        normed_own = normalize(whole_rows, gain_row)
        normed = lax.all_gather(normed_own, "dp", axis=0, tiled=True)
        active = encode_every(normed, encoder, biases, list_ids, slot_live)

        def self_term(first_row, row_count):
            return jnp.dot(active, decoder, preferred_element_type=jnp.float32)

        def cross_term(first_row, row_count):
            return jnp.dot(active, dec_cross, preferred_element_type=jnp.float32)

        recon_share = reduce_owners(self_term, own_rows)
        cross_share = reduce_owners(cross_term, own_rows)
        output = (recon_share + carried).astype(jnp.bfloat16)
        outputs.append(output)
        if step_index < batch_count:
            following = (current.astype(jnp.float32) + output.astype(jnp.float32)).astype(
                jnp.bfloat16
            )
            held_wide, carried = passed_along(
                (following.astype(jnp.float32), cross_share), "segment", 1
            )
            held_resid = held_wide.astype(jnp.bfloat16)
    stacked = jnp.stack(
        [
            jnp.where(is_first, outputs[batch_index], outputs[batch_index + 1])
            for batch_index in range(batch_count)
        ]
    )
    return stacked[None]


def solution(mesh):
    return jax.shard_map(
        body,
        mesh=mesh,
        in_specs=(
            P(None, "dp", "latent"),
            P("segment", None),
            P("segment", None, ("latent", "dp")),
            P("segment", ("latent", "dp")),
            P("segment", ("latent", "dp"), None),
            P(("latent", "dp"), None),
            P("segment", None, None, ("latent", "dp"), None),
            P("segment", None, None, ("latent", "dp")),
        ),
        out_specs=P("segment", None, "dp", "latent"),
        check_vma=False,
    )
```

profile of v0, /device:TPU:32, one launch (start us, length us, event | category | flops | bytes accessed | tf_op | source)
XLA Modules:
  0.0 1253.8 jit_solution(16589999895047764935)
XLA Ops:
  10.0 26.8 %all-gather = bf16[1,16,3584]{1,0,2:T(2,128)(2,1)S(1)} all-gather(bf16[1,16,224]{1,0,2:T(2,128)(2,1)S(1)} %get-tuple-element.17), channel_id=2, replica_groups=mesh['segment'=2,'latent'=16,'dp'=8] {'latent'}, dimensions={2}, use_global_device_ids=true | all-gather | bytes 121856 | tf_op jit(solution)/shard_map/all_gather | solution.py:66
  38.9 29.2 %all_gather.31 = bf16[128,3584]{1,0:T(8,128)(2,1)S(1)} all-gather(bf16[16,3584]{1,0:T(8,128)(2,1)S(1)} %fusion.84), channel_id=1, replica_groups=mesh['segment'=2,'latent'=16,'dp'=8] {'dp'}, dimensions={0}, use_global_device_ids=true | all-gather | bytes 1032192 | tf_op jit(solution)/shard_map/all_gather | solution.py:68
  72.8 38.7 %reduce-scatter.37.cloned.1.call-done = f32[16,3584]{1,0:T(8,128)} async-done(((f32[128,3584]{1,0:T(8,128)}), f32[16,3584]{1,0:T(8,128)}) %reduce-scatter.37.cloned.1.call-update) | async-done | bytes 229392 | tf_op jit(solution)/shard_map/reduce_scatter | solution.py:36
  118.5 74.9 %reduce-scatter.55.cloned.1.call-done = f32[224,16]{1,0:T(8,128)} async-done(((f32[3584,16]{1,0:T(8,128)}), f32[224,16]{1,0:T(8,128)}) %reduce-scatter.55.cloned.1.call-update) | async-done | bytes 14352
  196.5 22.9 %all-gather.1 = bf16[16,224,16]{1,2,0:T(8,128)(2,1)S(1)} all-gather(bf16[1,224,16]{1,2,0:T(8,128)(2,1)S(1)} %copy.91), channel_id=1, replica_groups=mesh['segment'=2,'latent'=16,'dp'=8] {'latent'}, dimensions={0}, use_global_device_ids=true | all-gather | bytes 121856 | tf_op jit(solution)/shard_map/all_gather | solution.py:66
  219.9 28.9 %all_gather.33 = bf16[128,3584]{1,0:T(8,128)(2,1)S(1)} all-gather(bf16[16,3584]{1,0:T(8,128)(2,1)S(1)} %fusion.87), channel_id=1, replica_groups=mesh['segment'=2,'latent'=16,'dp'=8] {'dp'}, dimensions={0}, use_global_device_ids=true | all-gather | bytes 1032192 | tf_op jit(solution)/shard_map/all_gather | solution.py:68
  256.3 36.2 %reduce-scatter.39.cloned.1.call-done = f32[16,3584]{1,0:T(8,128)} async-done(((f32[128,3584]{1,0:T(8,128)}), f32[16,3584]{1,0:T(8,128)}) %reduce-scatter.39.cloned.1.call-update) | async-done | bytes 229392 | tf_op jit(solution)/shard_map/reduce_scatter | solution.py:36
  299.3 75.0 %reduce-scatter.59.cloned.1.call-done = f32[224,16]{1,0:T(8,128)} async-done(((f32[3584,16]{1,0:T(8,128)}), f32[224,16]{1,0:T(8,128)}) %reduce-scatter.59.cloned.1.call-update) | async-done | bytes 14352
  376.8 79.3 %reduce-scatter.57.cloned.1.call-done = f32[224,16]{1,0:T(8,128)} async-done(((f32[3584,16]{1,0:T(8,128)}), f32[224,16]{1,0:T(8,128)}) %reduce-scatter.57.cloned.1.call-update) | async-done | bytes 14352
  459.3 23.0 %all-gather.2 = bf16[16,224,16]{1,2,0:T(8,128)(2,1)S(1)} all-gather(bf16[1,224,16]{1,2,0:T(8,128)(2,1)S(1)} %copy.96), channel_id=1, replica_groups=mesh['segment'=2,'latent'=16,'dp'=8] {'latent'}, dimensions={0}, use_global_device_ids=true | all-gather | bytes 121856 | tf_op jit(solution)/shard_map/all_gather | solution.py:66
  482.8 28.4 %all_gather.35 = bf16[128,3584]{1,0:T(8,128)(2,1)S(1)} all-gather(bf16[16,3584]{1,0:T(8,128)(2,1)S(1)} %fusion.88), channel_id=1, replica_groups=mesh['segment'=2,'latent'=16,'dp'=8] {'dp'}, dimensions={0}, use_global_device_ids=true | all-gather | bytes 1032192 | tf_op jit(solution)/shard_map/all_gather | solution.py:68
  518.7 36.9 %reduce-scatter.43.cloned.1.call-done = f32[16,3584]{1,0:T(8,128)} async-done(((f32[128,3584]{1,0:T(8,128)}), f32[16,3584]{1,0:T(8,128)}) %reduce-scatter.43.cloned.1.call-update) | async-done | bytes 229392 | tf_op jit(solution)/shard_map/reduce_scatter | solution.py:36
  562.4 74.8 %reduce-scatter.63.cloned.1.call-done = f32[224,16]{1,0:T(8,128)} async-done(((f32[3584,16]{1,0:T(8,128)}), f32[224,16]{1,0:T(8,128)}) %reduce-scatter.63.cloned.1.call-update) | async-done | bytes 14352
  639.7 79.3 %reduce-scatter.61.cloned.1.call-done = f32[224,16]{1,0:T(8,128)} async-done(((f32[3584,16]{1,0:T(8,128)}), f32[224,16]{1,0:T(8,128)}) %reduce-scatter.61.cloned.1.call-update) | async-done | bytes 14352
  722.2 23.1 %all-gather.3 = bf16[16,224,16]{1,2,0:T(8,128)(2,1)S(1)} all-gather(bf16[1,224,16]{1,2,0:T(8,128)(2,1)S(1)} %copy.101), channel_id=1, replica_groups=mesh['segment'=2,'latent'=16,'dp'=8] {'latent'}, dimensions={0}, use_global_device_ids=true | all-gather | bytes 121856 | tf_op jit(solution)/shard_map/all_gather | solution.py:66
  745.8 28.6 %all_gather.37 = bf16[128,3584]{1,0:T(8,128)(2,1)S(1)} all-gather(bf16[16,3584]{1,0:T(8,128)(2,1)S(1)} %fusion.89), channel_id=1, replica_groups=mesh['segment'=2,'latent'=16,'dp'=8] {'dp'}, dimensions={0}, use_global_device_ids=true | all-gather | bytes 1032192 | tf_op jit(solution)/shard_map/all_gather | solution.py:68
  782.0 36.4 %reduce-scatter.47.cloned.1.call-done = f32[16,3584]{1,0:T(8,128)} async-done(((f32[128,3584]{1,0:T(8,128)}), f32[16,3584]{1,0:T(8,128)}) %reduce-scatter.47.cloned.1.call-update) | async-done | bytes 229392 | tf_op jit(solution)/shard_map/reduce_scatter | solution.py:36
  825.1 75.2 %reduce-scatter.67.cloned.1.call-done = f32[224,16]{1,0:T(8,128)} async-done(((f32[3584,16]{1,0:T(8,128)}), f32[224,16]{1,0:T(8,128)}) %reduce-scatter.67.cloned.1.call-update) | async-done | bytes 14352
  902.7 79.3 %reduce-scatter.65.cloned.1.call-done = f32[224,16]{1,0:T(8,128)} async-done(((f32[3584,16]{1,0:T(8,128)}), f32[224,16]{1,0:T(8,128)}) %reduce-scatter.65.cloned.1.call-update) | async-done | bytes 14352
  985.3 23.0 %all-gather.4 = bf16[16,224,16]{1,2,0:T(8,128)(2,1)S(1)} all-gather(bf16[1,224,16]{1,2,0:T(8,128)(2,1)S(1)} %copy.105), channel_id=1, replica_groups=mesh['segment'=2,'latent'=16,'dp'=8] {'latent'}, dimensions={0}, use_global_device_ids=true | all-gather | bytes 121856 | tf_op jit(solution)/shard_map/all_gather | solution.py:66
  1008.7 28.5 %all_gather.39 = bf16[128,3584]{1,0:T(8,128)(2,1)S(1)} all-gather(bf16[16,3584]{1,0:T(8,128)(2,1)S(1)} %fusion.90), channel_id=1, replica_groups=mesh['segment'=2,'latent'=16,'dp'=8] {'dp'}, dimensions={0}, use_global_device_ids=true | all-gather | bytes 1032192 | tf_op jit(solution)/shard_map/all_gather | solution.py:68
  1045.7 36.4 %reduce-scatter.51.cloned.1.call-done = f32[16,3584]{1,0:T(8,128)} async-done(((f32[128,3584]{1,0:T(8,128)}), f32[16,3584]{1,0:T(8,128)}) %reduce-scatter.51.cloned.1.call-update) | async-done | bytes 229392 | tf_op jit(solution)/shard_map/reduce_scatter | solution.py:36
  1084.8 78.7 %reduce-scatter.71.cloned.1.call-done = f32[224,16]{1,0:T(8,128)} async-done(((f32[3584,16]{1,0:T(8,128)}), f32[224,16]{1,0:T(8,128)}) %reduce-scatter.71.cloned.1.call-update) | async-done | bytes 14352
  1166.0 79.3 %reduce-scatter.69.cloned.1.call-done = f32[224,16]{1,0:T(8,128)} async-done(((f32[3584,16]{1,0:T(8,128)}), f32[224,16]{1,0:T(8,128)}) %reduce-scatter.69.cloned.1.call-update) | async-done | bytes 14352
  (169 shorter events, 96.9 us)
Async XLA Ops:
  6.5 105.0 %reduce-scatter.37.cloned.1.call-start = ((), (), s32[]{:S(2)}) async-start(), calls=%async_computation.18 | async-start | bytes 2064384 | tf_op jit(solution)/shard_map/reduce_scatter | solution.py:36
  72.8 120.6 %reduce-scatter.55.cloned.1.call-start = ((), (), s32[]{:S(2)}) async-start(), calls=%async_computation.27 | async-start | bytes 1949696
  114.3 139.2 %reduce-scatter.41.cloned.1.call-start = ((), (), s32[]{:S(2)}) async-start(), calls=%async_computation.20 | async-start | bytes 2064384 | tf_op jit(solution)/shard_map/reduce_scatter | solution.py:36
  118.3 174.2 %reduce-scatter.39.cloned.1.call-start = ((), (), s32[]{:S(2)}) async-start(), calls=%async_computation.19 | async-start | bytes 2064384 | tf_op jit(solution)/shard_map/reduce_scatter | solution.py:36
  253.4 120.9 %reduce-scatter.59.cloned.1.call-start = ((), (), s32[]{:S(2)}) async-start(), calls=%async_computation.29 | async-start | bytes 1949696
  256.3 199.9 %reduce-scatter.57.cloned.1.call-start = ((), (), s32[]{:S(2)}) async-start(), calls=%async_computation.28 | async-start | bytes 1949696
  295.3 220.6 %reduce-scatter.45.cloned.1.call-start = ((), (), s32[]{:S(2)}) async-start(), calls=%async_computation.22 | async-start | bytes 2064384 | tf_op jit(solution)/shard_map/reduce_scatter | solution.py:36
  299.3 256.3 %reduce-scatter.43.cloned.1.call-start = ((), (), s32[]{:S(2)}) async-start(), calls=%async_computation.21 | async-start | bytes 2064384 | tf_op jit(solution)/shard_map/reduce_scatter | solution.py:36
  374.4 2.4 collective-permute-start.1
  457.1 2.2 collective-permute-start.2
  515.9 121.4 %reduce-scatter.63.cloned.1.call-start = ((), (), s32[]{:S(2)}) async-start(), calls=%async_computation.31 | async-start | bytes 1949696
  518.7 200.3 %reduce-scatter.61.cloned.1.call-start = ((), (), s32[]{:S(2)}) async-start(), calls=%async_computation.30 | async-start | bytes 1949696
  558.4 220.8 %reduce-scatter.49.cloned.1.call-start = ((), (), s32[]{:S(2)}) async-start(), calls=%async_computation.24 | async-start | bytes 2064384 | tf_op jit(solution)/shard_map/reduce_scatter | solution.py:36
  562.4 256.0 %reduce-scatter.47.cloned.1.call-start = ((), (), s32[]{:S(2)}) async-start(), calls=%async_computation.23 | async-start | bytes 2064384 | tf_op jit(solution)/shard_map/reduce_scatter | solution.py:36
  637.2 2.4 collective-permute-start.3
  720.0 2.2 collective-permute-start.4
  779.1 121.2 %reduce-scatter.67.cloned.1.call-start = ((), (), s32[]{:S(2)}) async-start(), calls=%async_computation.33 | async-start | bytes 1949696
  781.9 200.2 %reduce-scatter.65.cloned.1.call-start = ((), (), s32[]{:S(2)}) async-start(), calls=%async_computation.32 | async-start | bytes 1949696
  821.1 221.8 %reduce-scatter.53.cloned.1.call-start = ((), (), s32[]{:S(2)}) async-start(), calls=%async_computation.26 | async-start | bytes 2064384 | tf_op jit(solution)/shard_map/reduce_scatter | solution.py:36
  825.1 257.0 %reduce-scatter.51.cloned.1.call-start = ((), (), s32[]{:S(2)}) async-start(), calls=%async_computation.25 | async-start | bytes 2064384 | tf_op jit(solution)/shard_map/reduce_scatter | solution.py:36
  900.3 2.4 collective-permute-start.5
  1042.8 120.7 %reduce-scatter.71.cloned.1.call-start = ((), (), s32[]{:S(2)}) async-start(), calls=%async_computation.35 | async-start | bytes 1949696
  1045.7 199.6 %reduce-scatter.69.cloned.1.call-start = ((), (), s32[]{:S(2)}) async-start(), calls=%async_computation.34 | async-start | bytes 1949696
  1163.5 2.4 collective-permute-start.7
  (9 other events, 385.8 us)
Sparse Core Ops, SparseCore 0:
  72.9 38.5 reduce-scatter.36
  115.1 78.2 reduce-scatter.54
  195.9 41.7 reduce-scatter.40
  253.6 38.9 reduce-scatter.38
  295.9 78.3 reduce-scatter.58
  377.7 78.3 reduce-scatter.56
  458.7 41.9 reduce-scatter.44
  516.0 39.5 reduce-scatter.42
  559.1 78.0 reduce-scatter.62
  640.6 78.3 reduce-scatter.60
  721.6 41.9 reduce-scatter.48
  779.2 39.0 reduce-scatter.46
  821.9 78.3 reduce-scatter.66
  903.7 78.3 reduce-scatter.64
  984.5 41.7 reduce-scatter.52
  1043.0 39.0 reduce-scatter.50
  1085.5 78.0 reduce-scatter.70
  1166.9 78.3 reduce-scatter.68
where the time goes:
time: 1250 us
  waiting for transfers between devices  887 us (71%)
  blocking collectives  262 us (21%)
  matrix products  39.8 us (3%)
  local copies, waits for them, and re-layouts  32.2 us (3%)
  between operations  14.1 us (1%)
    unnamed x27, waiting for transfers between devices  696 us
    reduce_scatter x9, waiting for transfers between devices, reduce_owners(): lax.psum_scatter(term_rows(jnp.int32(0), own_rows * lax.axis_size('dp')),...  185 us
    all_gather x5, blocking collectives, body(): normed = lax.all_gather(normed_own, 'dp', axis=0, tiled=True)  144 us
    all_gather x5, blocking collectives, body(): whole_rows = lax.all_gather(current, 'latent', axis=1, tiled=True)  119 us
    unnamed x30, local copies, waits for them, and re-layouts  25.2 us
  transfers between devices with their start and end apart: 26, of which 22 were waited for; matrix products, arithmetic and copies ran while one was open for 5% of the time, Pallas kernels for 0%

commit v1 on v0

v1 whole, which is shorter than its diff:
```python
import jax
import jax.numpy as jnp
from jax import lax
from jax.sharding import PartitionSpec as P

BLK_DEV = 8
BLOCK = 64

norm_eps = 1e-06


def swapped(value):
    return lax.ppermute(value, "segment", [(0, 1), (1, 0)])


def exchanged(value, axis):
    return lax.all_to_all(value, axis, 0, 0)


def spread(value, axis):
    count = lax.axis_size(axis)
    return exchanged(jnp.broadcast_to(value[None], (count,) + value.shape), axis)


def normalize(resid, gain_row):
    values = resid.astype(jnp.float32)
    scaling = lax.rsqrt(jnp.mean(values * values, axis=-1, keepdims=True) + norm_eps)
    return (values * scaling * gain_row).astype(jnp.bfloat16)


def summed(parts):
    return jnp.sum(parts.astype(jnp.float32), axis=0).astype(jnp.bfloat16)


def body(resid_in, norm_gain, enc_weight, enc_bias, dec_self, dec_cross, block_ids, block_counts):
    segment_index = lax.axis_index("segment")
    is_first = segment_index == 0
    latents = lax.axis_size("latent")
    dps = lax.axis_size("dp")
    batches, own_rows, own_cols = resid_in.shape
    half = batches // 2
    cols = latents * own_cols
    width = enc_weight.shape[2]
    pair = half * own_rows // latents
    rows = half * own_rows * dps

    list_ids = block_ids[0, :, :, 0, :]
    counts = block_counts[0, :, :, 0]
    slot_live = jnp.arange(list_ids.shape[-1], dtype=jnp.int32) < counts[..., None]
    matches = (list_ids[..., None] == jnp.arange(BLK_DEV, dtype=jnp.int32)) & slot_live[..., None]
    live_own = jnp.any(matches, axis=2).astype(jnp.float32)
    tiles = live_own.shape[1]

    small_own = jnp.concatenate([norm_gain[0], enc_bias[0], live_own.reshape(-1)])
    enc_other = swapped(enc_weight[0])
    dec_other = swapped(dec_self[0])
    small_other = swapped(small_own)

    def layered(own, other):
        return jnp.where(is_first, own, other), jnp.where(is_first, other, own)

    enc = layered(enc_weight[0], enc_other)
    dec = layered(dec_self[0], dec_other)
    small = layered(small_own, small_other)

    def parts_of(values):
        gain = values[:cols]
        bias = values[cols : cols + width]
        live = values[cols + width :].reshape(batches, tiles, BLK_DEV)
        live = lax.dynamic_slice_in_dim(live, segment_index * half, half, 0)
        live = jnp.broadcast_to(
            live[:, None, :, None, :, None],
            (half, latents // half, tiles, dps // tiles * pair, BLK_DEV, BLOCK),
        )
        return gain, bias, live.reshape(rows, width)

    def encode(normed, layer):
        _, bias, live = parts_of(small[layer])
        before = jnp.dot(normed, enc[layer], preferred_element_type=jnp.float32) + bias
        return (jnp.maximum(before, 0.0) * live).astype(jnp.bfloat16)

    mine = lax.dynamic_slice_in_dim(resid_in, segment_index * half, half, 0)
    by_dp = spread(mine, "dp").reshape(dps, latents, pair, own_cols)
    by_row = by_dp.transpose(1, 0, 2, 3).reshape(rows, own_cols)
    resid0 = spread(by_row, "latent").transpose(1, 0, 2).reshape(rows, cols)

    active0 = encode(normalize(resid0, small[0][:cols]), 0)
    partial0 = jnp.dot(active0, dec[0], preferred_element_type=jnp.float32).astype(jnp.bfloat16)
    share0 = summed(exchanged(partial0.reshape(latents, dps * pair, cols), "latent"))
    recon0 = summed(exchanged(share0.reshape(dps, pair, cols), "dp"))
    first_row = (lax.axis_index("latent") * dps + lax.axis_index("dp")) * pair
    own_resid0 = lax.dynamic_slice_in_dim(resid0, first_row, pair, 0)
    resid1 = (own_resid0.astype(jnp.float32) + recon0.astype(jnp.float32)).astype(jnp.bfloat16)
    normed1_own = normalize(resid1, small[1][:cols])
    normed1_some = spread(normed1_own, "dp").reshape(dps * pair, cols)
    normed1 = spread(normed1_some, "latent").reshape(rows, cols)

    active1 = encode(normed1, 1)
    partial1 = (
        jnp.dot(active1, dec[1], preferred_element_type=jnp.float32)
        + jnp.dot(active0, dec_cross, preferred_element_type=jnp.float32)
    ).astype(jnp.bfloat16)
    outgoing = jnp.concatenate([partial1, recon0], axis=0)
    outgoing = outgoing.reshape(rows + pair, latents, own_cols).transpose(1, 0, 2)
    incoming = exchanged(outgoing, "latent")
    share1 = summed(incoming[:, :rows]).reshape(latents, dps, pair, own_cols)
    share1 = share1.transpose(1, 0, 2, 3).reshape(dps, latents * pair, own_cols)
    recon1 = summed(exchanged(share1, "dp")).reshape(half, own_rows, own_cols)
    recon0_mine = incoming[:, rows:].reshape(half, own_rows, own_cols)
    other = swapped(jnp.where(is_first, recon1, recon0_mine))
    first = jnp.where(is_first, recon0_mine, other)
    second = jnp.where(is_first, other, recon1)
    return jnp.concatenate([first, second], axis=0)[None]


def solution(mesh):
    return jax.shard_map(
        body,
        mesh=mesh,
        in_specs=(
            P(None, "dp", "latent"),
            P("segment", None),
            P("segment", None, ("latent", "dp")),
            P("segment", ("latent", "dp")),
            P("segment", ("latent", "dp"), None),
            P(("latent", "dp"), None),
            P("segment", None, None, ("latent", "dp"), None),
            P("segment", None, None, ("latent", "dp")),
        ),
        out_specs=P("segment", None, "dp", "latent"),
        check_vma=False,
    )
```

time: 1250 us -> 213 us (0.17)
  waiting for transfers between devices: 887 us -> 88.4 us
  blocking collectives: 262 us -> 55.9 us
  matrix products: 39.8 us -> 19.9 us
  local copies, waits for them, and re-layouts: 32.2 us -> 14.7 us
  starting transfers between devices: 11 us -> 25.7 us
  between operations: 14.1 us -> 0.35 us
    unnamed x27 -> x0, waiting for transfers between devices: 696 us -> none
    all_gather x10 -> x0, blocking collectives: 262 us -> none  [the longest x5 144 us: body(): normed = lax.all_gather(normed_own, 'dp', axis=0, tiled=True)]
    reduce_scatter x9 -> x0, waiting for transfers between devices: 185 us -> none  [reduce_owners(): lax.psum_scatter(term_rows(jnp.int32(0), own_rows * lax.axis_size('dp')),...]
    all_to_all x0 -> x5, waiting for transfers between devices: none -> 86.1 us  [exchanged(): return lax.all_to_all(value, axis, 0, 0)]
    all_to_all x0 -> x3, blocking collectives: none -> 55.9 us  [exchanged(): return lax.all_to_all(value, axis, 0, 0)]
    all_to_all x0 -> x5, starting transfers between devices: none -> 25 us  [exchanged(): return lax.all_to_all(value, axis, 0, 0)]
    unnamed x30 -> x19, local copies, waits for them, and re-layouts: 25.2 us -> 1.38 us
    dot_general x13 -> x5, matrix products: 39.8 us -> 19.9 us  [the longest x2 8.88 us: encode(): jnp.dot(normed, enc[layer], preferred_element_type=jnp.float32) + bias]
  transfers between devices with their start and end apart: 26 -> 9, of which waited for: 22 -> 7; matrix products, arithmetic and copies ran while one was open for 5% -> 8% of each run, Pallas kernels for 0% -> 0%
where the time goes in v1:
time: 213 us; the launch traced here: 210 us
  waiting for transfers between devices  88.4 us (42%)
  blocking collectives  55.9 us (26%)
  starting transfers between devices  25.7 us (12%)
  matrix products  19.9 us (9%)
  local copies, waits for them, and re-layouts  14.7 us (7%)
  other arithmetic  5.26 us (2%)
    all_to_all x5, waiting for transfers between devices, exchanged(): return lax.all_to_all(value, axis, 0, 0)  86.1 us
    all_to_all x3, blocking collectives, exchanged(): return lax.all_to_all(value, axis, 0, 0)  55.9 us
    all_to_all x5, starting transfers between devices, exchanged(): return lax.all_to_all(value, axis, 0, 0)  25 us
    dot_general x2, matrix products, encode(): jnp.dot(normed, enc[layer], preferred_element_type=jnp.float32) + bias  8.88 us
    dot_general x1, matrix products, body(): jnp.dot(active0, dec_cross, preferred_element_type=jnp.float32)  5.12 us
    reshape x2, local copies, waits for them, and re-layouts, body(): outgoing.reshape(rows + pair, latents, own_cols).transpose(1, 0, 2)  5.11 us
  transfers between devices with their start and end apart: 9, of which 7 were waited for; matrix products, arithmetic and copies ran while one was open for 8% of the time, Pallas kernels for 0%

profile of v1, /device:TPU:32, one launch (start us, length us, event | category | flops | bytes accessed | tf_op | source)
XLA Modules:
  0.0 210.2 jit_solution(4511889908151359073)
XLA Ops:
  0.8 16.1 %all_to_all.40 = bf16[8,2,16,224]{3,2,1,0:T(8,128)(2,1)S(1)} all-to-all(bf16[8,2,16,224]{3,2,1,0:T(8,128)(2,1)S(1)} %broadcast_in_dim.18), channel_id=1, replica_groups=mesh['segment'=2,'latent'=16,'dp'=8] {'dp'}, dimensions={0} | all-to-all | bytes 229376 | tf_op jit(solution)/shard_map/all_to_all | solution.py:17
  17.3 1.5 broadcast_in_dim.20
  18.8 7.0 %all-to-all-start.1 = ((bf16[16,256,224]{1,2,0:T(8,128)(2,1)}), bf16[16,256,224]{1,2,0:T(8,128)(2,1)S(1)}, u32[]{:S(2)}, u32[]{:S(2)}) async-start(bf16[16,256,224]{1,2,0:T(8,128)(2,1)} %broadcast_in_dim.20), calls=%async_computation.1 | async-start | bytes 3670016 | tf_op jit(solution)/shard_map/all_to_all | solution.py:17
  26.4 1.2 collective-permute-done
  29.1 22.1 %all-to-all-done.1 = bf16[16,256,224]{1,2,0:T(8,128)(2,1)S(1)} async-done(((bf16[16,256,224]{1,2,0:T(8,128)(2,1)}), bf16[16,256,224]{1,2,0:T(8,128)(2,1)S(1)}, u32[]{:S(2)}, u32[]{:S(2)}) %all-to-all-start.1) | async-done | bytes 1835040 | tf_op jit(solution)/shard_map/all_to_all | solution.py:17
  51.7 4.5 %fusion.34 = bf16[256,512]{1,0:T(8,128)(2,1)S(1)} fusion(f32[256,512]{1,0:T(8,128)} %reshape.91, bf16[3584,512]{1,0:T(8,128)(2,1)} %collective-permute-done.1, pred[]{:T(512)S(6)} %eq.18, bf16[256,3584]{0,1:T(8,128)(2,1)S(1)} %bitcast.47, f32[3584]{0:T(1024)S(1)} %slice.54, f32[256]{0:T(256)S(1)} %add_rsqrt_fusion, f32[512]{0:T(512)S(1)} %slice.55, ...), kind=kOutput, calls=%fused_computation.27 | convolution fusion | flops 945553408 | bytes 9978881 | tf_op jit(solution)/shard_map/dot_general | solution.py:79
  56.2 2.4 %convolution_convert_fusion = bf16[256,3584]{1,0:T(8,128)(2,1)} fusion(bf16[256,512]{1,0:T(8,128)(2,1)S(1)} %fusion.34, bf16[512,3584]{1,0:T(8,128)(2,1)} %collective-permute-done.2, pred[]{:T(512)S(6)} %eq.18, bf16[1,512,3584]{2,1,0:T(8,128)(2,1)S(1)} %copy-done.2), kind=kOutput, calls=%fused_computation.2 | convolution fusion | flops 942276608 | bytes 9437185 | tf_op jit(solution)/shard_map/dot_general | solution.py:88
  58.6 4.4 %all-to-all-start.2 = ((bf16[16,16,3584]{2,1,0:T(8,128)(2,1)}), bf16[16,16,3584]{2,1,0:T(8,128)(2,1)}, u32[]{:S(2)}, u32[]{:S(2)}) async-start(bf16[16,16,3584]{2,1,0:T(8,128)(2,1)} %bitcast.51), calls=%async_computation.2 | async-start | bytes 3670016 | tf_op jit(solution)/shard_map/all_to_all | solution.py:17
  63.1 31.3 %all-to-all-done.2 = bf16[16,16,3584]{2,1,0:T(8,128)(2,1)} async-done(((bf16[16,16,3584]{2,1,0:T(8,128)(2,1)}), bf16[16,16,3584]{2,1,0:T(8,128)(2,1)}, u32[]{:S(2)}, u32[]{:S(2)}) %all-to-all-start.2) | async-done | bytes 1835040 | tf_op jit(solution)/shard_map/all_to_all | solution.py:17
  94.4 1.7 reduce_sum.67
  96.8 4.9 %all-to-all-start.3 = ((bf16[8,2,3584]{2,1,0:T(2,128)(2,1)}), bf16[8,2,3584]{2,1,0:T(2,128)(2,1)S(1)}, u32[]{:S(2)}, u32[]{:S(2)}) async-start(bf16[8,2,3584]{2,1,0:T(2,128)(2,1)} %reshape.93), calls=%async_computation.3 | async-start | bytes 229376 | tf_op jit(solution)/shard_map/all_to_all | solution.py:17
  102.3 7.1 %all-to-all-done.3 = bf16[8,2,3584]{2,1,0:T(2,128)(2,1)S(1)} async-done(((bf16[8,2,3584]{2,1,0:T(2,128)(2,1)}), bf16[8,2,3584]{2,1,0:T(2,128)(2,1)S(1)}, u32[]{:S(2)}, u32[]{:S(2)}) %all-to-all-start.3) | async-done | bytes 114720 | tf_op jit(solution)/shard_map/all_to_all | solution.py:17
  109.9 11.3 %all_to_all.41 = bf16[8,2,3584]{2,1,0:T(2,128)(2,1)S(1)} all-to-all(bf16[8,2,3584]{2,1,0:T(2,128)(2,1)S(1)} %broadcast_in_dim.22), channel_id=1, replica_groups=mesh['segment'=2,'latent'=16,'dp'=8] {'dp'}, dimensions={0} | all-to-all | bytes 229376 | tf_op jit(solution)/shard_map/all_to_all | solution.py:17
  121.2 1.4 broadcast_in_dim.24
  122.6 3.9 %all-to-all-start.5 = ((bf16[16,16,3584]{2,1,0:T(8,128)(2,1)}), bf16[16,16,3584]{2,1,0:T(8,128)(2,1)S(1)}, u32[]{:S(2)}, u32[]{:S(2)}) async-start(bf16[16,16,3584]{2,1,0:T(8,128)(2,1)} %broadcast_in_dim.24), calls=%async_computation.5 | async-start | bytes 3670016 | tf_op jit(solution)/shard_map/all_to_all | solution.py:17
  127.8 5.1 %fusion.46 = f32[256,3584]{1,0:T(8,128)} fusion(bf16[256,512]{1,0:T(8,128)(2,1)S(1)} %fusion.34, bf16[512,3584]{1,0:T(8,128)(2,1)} %param.13), kind=kOutput, calls=%fused_computation.55 | convolution fusion | flops 939524096 | bytes 7602176 | tf_op jit(solution)/shard_map/dot_general | solution.py:101
  132.9 17.9 %all-to-all-done.5 = bf16[16,16,3584]{2,1,0:T(8,128)(2,1)S(1)} async-done(((bf16[16,16,3584]{2,1,0:T(8,128)(2,1)}), bf16[16,16,3584]{2,1,0:T(8,128)(2,1)S(1)}, u32[]{:S(2)}, u32[]{:S(2)}) %all-to-all-start.5) | async-done | bytes 1835040 | tf_op jit(solution)/shard_map/all_to_all | solution.py:17
  150.9 4.4 %fusion.31 = bf16[256,512]{1,0:T(8,128)(2,1)S(1)} fusion(f32[256,512]{1,0:T(8,128)S(1)} %copy-done.4, bf16[256,3584]{1,0:T(8,128)(2,1)S(1)} %bitcast.52, bf16[3584,512]{1,0:T(8,128)(2,1)} %collective-permute-done.1, pred[]{:T(512)S(6)} %eq.18, f32[512]{0:T(512)S(1)} %slice.58, bf16[1,3584,512]{2,1,0:T(8,128)(2,1)} %param.10), kind=kOutput, calls=%fused_computation.26 | convolution fusion | flops 941883392 | bytes 9963521 | tf_op jit(solution)/shard_map/dot_general | solution.py:79
  156.2 3.5 %fusion = bf16[256,3584]{1,0:T(8,128)(2,1)S(1)} fusion(f32[256,3584]{1,0:T(8,128)S(1)} %copy-done.1, bf16[256,512]{1,0:T(8,128)(2,1)S(1)} %fusion.31, bf16[512,3584]{1,0:T(8,128)(2,1)} %collective-permute-done.2, pred[]{:T(512)S(6)} %eq.18, bf16[1,512,3584]{2,1,0:T(8,128)(2,1)S(1)} %copy-done.3), kind=kOutput, calls=%fused_computation.1 | convolution fusion | flops 943194112 | bytes 13107201 | tf_op jit(solution)/shard_map/dot_general | solution.py:100
  159.7 1.4 pad_maximum_fusion
  161.1 4.4 %reshape.96 = bf16[258,16,224]{2,1,0:T(8,128)(2,1)S(1)} reshape(bf16[258,3584]{1,0:T(8,128)(2,1)} %pad_maximum_fusion) | data formatting | bytes 3698688 | tf_op jit(solution)/shard_map/reshape | solution.py:104
  166.2 28.5 %all_to_all.42 = bf16[16,258,224]{2,1,0:T(8,128)(2,1)S(1)} all-to-all(bf16[16,258,224]{2,1,0:T(8,128)(2,1)S(1)} %bitcast.49), channel_id=1, replica_groups=mesh['segment'=2,'latent'=16,'dp'=8] {'latent'}, dimensions={0} | all-to-all | bytes 3698688 | tf_op jit(solution)/shard_map/all_to_all | solution.py:17
  195.8 4.8 %all-to-all-start.7 = ((bf16[8,32,224]{2,1,0:T(8,128)(2,1)}), bf16[8,32,224]{2,1,0:T(8,128)(2,1)S(1)}, u32[]{:S(2)}, u32[]{:S(2)}) async-start(bf16[8,32,224]{2,1,0:T(8,128)(2,1)} %copy.41), calls=%async_computation.7 | async-start | bytes 262144 | tf_op jit(solution)/shard_map/all_to_all | solution.py:17
  200.6 7.6 %all-to-all-done.7 = bf16[8,32,224]{2,1,0:T(8,128)(2,1)S(1)} async-done(((bf16[8,32,224]{2,1,0:T(8,128)(2,1)}), bf16[8,32,224]{2,1,0:T(8,128)(2,1)S(1)}, u32[]{:S(2)}, u32[]{:S(2)}) %all-to-all-start.7) | async-done | bytes 114720 | tf_op jit(solution)/shard_map/all_to_all | solution.py:17
  (74 shorter events, 11.4 us)
Async XLA Ops:
  0.0 0.8 copy-start
  0.0 25.9 %copy-start.8 = (s32[1,4,2,1]{1,3,2,0:T(1,128)S(1)}, s32[1,4,2,1]{1,3,2,0:T(1,128)}, u32[]{:S(2)}) copy-start(s32[1,4,2,1]{1,3,2,0:T(1,128)} %param.15) | copy-start | bytes 100
  0.0 26.0 %copy-start.7 = (s32[1,4,2,1,4]{4,3,2,1,0:T(1,128)S(1)}, s32[1,4,2,1,4]{4,3,2,1,0:T(1,128)}, u32[]{:S(2)}) copy-start(s32[1,4,2,1,4]{4,3,2,1,0:T(1,128)} %param.14) | copy-start | bytes 388
  0.0 26.2 %copy-start.5 = (f32[1,3584]{1,0:T(1,128)S(1)}, f32[1,3584]{1,0:T(1,128)}, u32[]{:S(2)}) copy-start(f32[1,3584]{1,0:T(1,128)} %param.9) | copy-start | bytes 43012
  0.0 26.3 %copy-start.6 = (f32[1,512]{1,0:T(1,128)S(1)}, f32[1,512]{1,0:T(1,128)}, u32[]{:S(2)}) copy-start(f32[1,512]{1,0:T(1,128)} %param.11) | copy-start | bytes 6148
  0.0 51.7 %collective-permute-start.1 = (bf16[3584,512]{1,0:T(8,128)(2,1)}, bf16[3584,512]{1,0:T(8,128)(2,1)}, u32[]{:S(2)}, u32[]{:S(2)}) collective-permute-start(bf16[3584,512]{1,0:T(8,128)(2,1)} %bitcast.62), channel_id=1, source_target_pairs={{0,128},{128,0},{1,129},{129,1},{2,130},{130,2},{3,131},{131,3},{4... | collective-permute-start | bytes 11010056 | tf_op jit(solution)/shard_map/ppermute | solution.py:13
  0.1 56.1 %collective-permute-start.2 = (bf16[512,3584]{1,0:T(8,128)(2,1)}, bf16[512,3584]{1,0:T(8,128)(2,1)}, u32[]{:S(2)}, u32[]{:S(2)}) collective-permute-start(bf16[512,3584]{1,0:T(8,128)(2,1)} %bitcast.50), channel_id=1, source_target_pairs={{0,128},{128,0},{1,129},{129,1},{2,130},{130,2},{3,131},{131,3},{4... | collective-permute-start | bytes 11010056 | tf_op jit(solution)/shard_map/ppermute | solution.py:13
  18.8 32.4 %all-to-all-start.1 = ((bf16[16,256,224]{1,2,0:T(8,128)(2,1)}), bf16[16,256,224]{1,2,0:T(8,128)(2,1)S(1)}, u32[]{:S(2)}, u32[]{:S(2)}) async-start(bf16[16,256,224]{1,2,0:T(8,128)(2,1)} %broadcast_in_dim.20), calls=%async_computation.1 | async-start | bytes 3670016 | tf_op jit(solution)/shard_map/all_to_all | solution.py:17
  26.3 1.3 collective-permute-start
  51.7 4.5 %copy-start.2 = (bf16[1,512,3584]{2,1,0:T(8,128)(2,1)S(1)}, bf16[1,512,3584]{2,1,0:T(8,128)(2,1)}, u32[]{:S(2)}) copy-start(bf16[1,512,3584]{2,1,0:T(8,128)(2,1)} %param.12) | copy-start | bytes 11010052
  58.6 35.7 %all-to-all-start.2 = ((bf16[16,16,3584]{2,1,0:T(8,128)(2,1)}), bf16[16,16,3584]{2,1,0:T(8,128)(2,1)}, u32[]{:S(2)}, u32[]{:S(2)}) async-start(bf16[16,16,3584]{2,1,0:T(8,128)(2,1)} %bitcast.51), calls=%async_computation.2 | async-start | bytes 3670016 | tf_op jit(solution)/shard_map/all_to_all | solution.py:17
  96.8 12.7 %all-to-all-start.3 = ((bf16[8,2,3584]{2,1,0:T(2,128)(2,1)}), bf16[8,2,3584]{2,1,0:T(2,128)(2,1)S(1)}, u32[]{:S(2)}, u32[]{:S(2)}) async-start(bf16[8,2,3584]{2,1,0:T(2,128)(2,1)} %reshape.93), calls=%async_computation.3 | async-start | bytes 229376 | tf_op jit(solution)/shard_map/all_to_all | solution.py:17
  122.6 28.3 %all-to-all-start.5 = ((bf16[16,16,3584]{2,1,0:T(8,128)(2,1)}), bf16[16,16,3584]{2,1,0:T(8,128)(2,1)S(1)}, u32[]{:S(2)}, u32[]{:S(2)}) async-start(bf16[16,16,3584]{2,1,0:T(8,128)(2,1)} %broadcast_in_dim.24), calls=%async_computation.5 | async-start | bytes 3670016 | tf_op jit(solution)/shard_map/all_to_all | solution.py:17
  127.8 23.1 %copy-start.4 = (f32[256,512]{1,0:T(8,128)S(1)}, f32[256,512]{1,0:T(8,128)}, u32[]{:S(2)}) copy-start(f32[256,512]{1,0:T(8,128)} %reshape.95) | copy-start | bytes 1572868
  150.9 4.4 %copy-start.1 = (f32[256,3584]{1,0:T(8,128)S(1)}, f32[256,3584]{1,0:T(8,128)}, u32[]{:S(2)}) copy-start(f32[256,3584]{1,0:T(8,128)} %fusion.46) | copy-start | bytes 11010052
  150.9 5.3 %copy-start.3 = (bf16[1,512,3584]{2,1,0:T(8,128)(2,1)S(1)}, bf16[1,512,3584]{2,1,0:T(8,128)(2,1)}, u32[]{:S(2)}) copy-start(bf16[1,512,3584]{2,1,0:T(8,128)(2,1)} %param.12) | copy-start | bytes 11010052
  195.8 12.4 %all-to-all-start.7 = ((bf16[8,32,224]{2,1,0:T(8,128)(2,1)}), bf16[8,32,224]{2,1,0:T(8,128)(2,1)S(1)}, u32[]{:S(2)}, u32[]{:S(2)}) async-start(bf16[8,32,224]{2,1,0:T(8,128)(2,1)} %copy.41), calls=%async_computation.7 | async-start | bytes 262144 | tf_op jit(solution)/shard_map/all_to_all | solution.py:17
  208.3 1.3 collective-permute-start.3

commit v2 on v1

v2 whole, which is shorter than its diff:
```python
import functools

import jax
import jax.numpy as jnp
from jax import lax
from jax.experimental import pallas as pl
from jax.experimental.pallas import tpu as pltpu
from jax.sharding import PartitionSpec as P

BLK_DEV = 8
BLOCK = 64
PIECES = 4

norm_eps = 1e-06

f32 = jnp.float32
bf16 = jnp.bfloat16


def swapped(value):
    return lax.ppermute(value, "segment", [(0, 1), (1, 0)])


def exchanged(value, axis):
    return lax.all_to_all(value, axis, 0, 0)


def spread(value, axis):
    count = lax.axis_size(axis)
    return exchanged(jnp.broadcast_to(value[None], (count,) + value.shape), axis)


def one_hot(shape, column_of_row):
    row = lax.broadcasted_iota(jnp.int32, shape, 0)
    column = lax.broadcasted_iota(jnp.int32, shape, 1)
    return (column == column_of_row(row)).astype(f32).astype(bf16)


def dot(left, right):
    return jnp.dot(left, right, preferred_element_type=f32)


def copies(source, target, sems, axis):
    size = target.shape[axis] // PIECES
    made = []
    for piece in range(PIECES):
        part = pl.ds(piece * size, size)
        index = (part, slice(None)) if axis == 0 else (slice(None), part)
        made.append(pltpu.make_async_copy(source.at[index], target.at[index], sems.at[piece]))
    return made


def start_from(choose_first, first, second, target, sems, axis):
    @pl.when(choose_first)
    def _():
        for copy in copies(first, target, sems, axis):
            copy.start()

    @pl.when(jnp.logical_not(choose_first))
    def _():
        for copy in copies(second, target, sems, axis):
            copy.start()

    return copies(first, target, sems, axis)


def first_layer(dps, pair, x_ref, gain_ref, bias_ref, live_ref, enc_own, enc_other, dec_own, dec_other,
                part_ref, active_ref, held_ref, enc, dec, enc_sems, dec_sems):
    latents, rows, own_cols = x_ref.shape
    cols = latents * own_cols
    group = rows // dps
    is_first = lax.axis_index("segment") == 0
    latent = lax.axis_index("latent")
    enc_copies = start_from(is_first, enc_own, enc_other, enc, enc_sems, 0)
    dec_copies = start_from(is_first, dec_own, dec_other, dec, dec_sems, 1)

    squares = jnp.zeros((rows, own_cols), f32)
    for piece in range(latents):
        values = x_ref[piece].astype(f32)
        squares += values * values
    scaling = lax.rsqrt(jnp.sum(squares, axis=1, keepdims=True) / cols + norm_eps)

    choose_own = one_hot(
        (dps * pair, rows), lambda row: (row // pair) * group + latent * pair + row % pair
    )
    total = jnp.zeros((rows, enc.shape[1]), f32)
    for piece in range(latents):
        if piece % (latents // PIECES) == 0:
            enc_copies[piece // (latents // PIECES)].wait()
        held_ref[piece] = dot(choose_own, x_ref[piece]).astype(bf16)
        normed = (x_ref[piece].astype(f32) * scaling * gain_ref[pl.ds(piece, 1), :]).astype(bf16)
        total += dot(normed, enc[pl.ds(piece * own_cols, own_cols), :])
    active = (jnp.maximum(total + bias_ref[...], 0.0) * live_ref[...].astype(f32)).astype(bf16)
    active_ref[...] = active
    to_owner = one_hot(
        (rows, rows),
        lambda row: ((row // pair) % dps) * group + row // (dps * pair) * pair + row % pair,
    )
    sorted_active = dot(to_owner, active).astype(bf16)
    size = cols // PIECES
    for piece in range(PIECES):
        dec_copies[piece].wait()
        part = pl.ds(piece * size, size)
        share = dot(sorted_active, dec[:, part]).astype(bf16)
        part_ref[:, :, part] = share.reshape(latents, rows // latents, size)


def second_layer(dps, pair, x_ref, active_ref, bias_ref, live_ref, recon_ref, enc_own, enc_other, dec_own, dec_other,
                 cross_hbm, out_ref, enc, dec, cross, enc_sems, dec_sems, cross_sems):
    latents = x_ref.shape[0]
    cols = x_ref.shape[2]
    rows = active_ref.shape[0]
    group = rows // dps
    own_cols = cols // latents
    is_first = lax.axis_index("segment") == 0
    enc_copies = start_from(is_first, enc_other, enc_own, enc, enc_sems, 0)
    dec_copies = start_from(is_first, dec_other, dec_own, dec, dec_sems, 1)
    cross_copies = copies(cross_hbm, cross, cross_sems, 1)
    for copy in cross_copies:
        copy.start()

    size = cols // PIECES
    total = jnp.zeros((rows, enc.shape[1]), f32)
    for piece in range(PIECES):
        enc_copies[piece].wait()
        part = pl.ds(piece * size, size)
        total += dot(x_ref[:, :, part].reshape(rows, size), enc[part, :])
    active = (jnp.maximum(total + bias_ref[...], 0.0) * live_ref[...].astype(f32)).astype(bf16)
    to_natural = one_hot(
        (rows, rows),
        lambda row: (row % group) // pair * (dps * pair) + row // group * pair + row % pair,
    )
    sorted_active = dot(to_natural, active).astype(bf16)
    earlier = active_ref[...]
    per_piece = latents // PIECES
    for piece in range(PIECES):
        dec_copies[piece].wait()
        cross_copies[piece].wait()
        part = pl.ds(piece * size, size)
        share = dot(sorted_active, dec[:, part]) + dot(earlier, cross[:, part])
        recon = recon_ref[:, part].astype(f32)
        for inner in range(per_piece):
            where = slice(inner * own_cols, (inner + 1) * own_cols)
            out_ref[piece * per_piece + inner, pl.ds(0, rows), :] = share[:, where].astype(bf16)
            out_ref[piece * per_piece + inner, pl.ds(rows, dps * pair), :] = recon[:, where].astype(bf16)


def sum_parts(x_ref, out_ref):
    total = x_ref[0].astype(f32)
    for source in range(1, x_ref.shape[0]):
        total += x_ref[source].astype(f32)
    _, height, width = out_ref.shape
    per_row = total.shape[1] // width
    for piece in range(out_ref.shape[0]):
        down, across = divmod(piece, per_row)
        out_ref[piece] = total[down * height : (down + 1) * height, across * width : (across + 1) * width]


def sum_and_spread(x_ref, out_ref):
    total = x_ref[0]
    for source in range(1, x_ref.shape[0]):
        total += x_ref[source]
    rounded = total.astype(bf16).astype(f32)
    for piece in range(out_ref.shape[0]):
        out_ref[piece] = rounded


def add_and_normalize(pieces_ref, held_ref, gain_ref, out_ref, recon_ref, wide):
    count, height, width = pieces_ref.shape
    cols = wide.shape[1]
    per_row = cols // width
    for piece in range(count):
        down, across = divmod(piece, per_row)
        wide[pl.ds(down * height, height), pl.ds(across * width, width)] = pieces_ref[piece]
    recon = wide[...]
    recon_ref[...] = recon.astype(bf16)
    resid = (held_ref[...].astype(f32) + recon).astype(bf16).astype(f32)
    scaling = lax.rsqrt(jnp.mean(resid * resid, axis=1, keepdims=True) + norm_eps)
    normed = (resid * scaling * gain_ref[...]).astype(bf16)
    for piece in range(out_ref.shape[0]):
        out_ref[piece] = normed


def sum_for_dp(rows, dps, pair, x_ref, out_ref):
    latents, taken, own_cols = x_ref.shape
    total = x_ref[0, pl.ds(0, rows), :].astype(f32)
    for source in range(1, latents):
        total += x_ref[source, pl.ds(0, rows), :].astype(f32)
    out_ref[1] = total.astype(bf16).reshape(dps, rows // dps, own_cols)
    extra = taken - rows
    dp = lax.axis_index("dp")
    choose_own = one_hot(
        (latents * pair, latents * extra),
        lambda row: (row // pair) * extra + dp * pair + row % pair,
    )
    recon = x_ref[:, pl.ds(rows, extra), :].reshape(latents * extra, own_cols)
    recon = dot(choose_own, recon).astype(bf16)
    for piece in range(dps):
        out_ref[0, piece] = recon


def finish(x_ref, out_ref):
    halves, dps = x_ref.shape[:2]
    is_first = lax.axis_index("segment") == 0
    dp = lax.axis_index("dp")
    for half in range(halves):
        total = x_ref[half, 0].astype(f32)
        for source in range(1, dps):
            total += x_ref[half, source].astype(f32)
        kept = x_ref[half, dp].astype(f32)
        out_ref[half] = jnp.where(is_first, kept, total).astype(bf16)


def call(kernel, outs, ins, hbm=0, scratch=(), limit=None):
    vmem = pl.BlockSpec(memory_space=pltpu.VMEM)
    single = not isinstance(outs, (list, tuple))
    return pl.pallas_call(
        kernel,
        out_shape=outs,
        in_specs=[vmem] * (len(ins) - hbm) + [pl.BlockSpec(memory_space=pl.ANY)] * hbm,
        out_specs=vmem if single else [vmem] * len(outs),
        scratch_shapes=list(scratch),
        compiler_params=pltpu.CompilerParams(vmem_limit_bytes=limit),
    )(*ins)


def array(shape, dtype=bf16):
    return jax.ShapeDtypeStruct(shape, dtype)


def body(resid_in, norm_gain, enc_weight, enc_bias, dec_self, dec_cross, block_ids, block_counts):
    segment_index = lax.axis_index("segment")
    is_first = segment_index == 0
    latents = lax.axis_size("latent")
    dps = lax.axis_size("dp")
    batches, own_rows, own_cols = resid_in.shape
    half = batches // 2
    cols = latents * own_cols
    width = enc_weight.shape[2]
    group = half * own_rows
    pair = group // latents
    some = dps * pair
    rows = group * dps

    list_ids = block_ids[0, :, :, 0, :]
    counts = block_counts[0, :, :, 0]
    slot_live = jnp.arange(list_ids.shape[-1], dtype=jnp.int32) < counts[..., None]
    matches = (list_ids[..., None] == jnp.arange(BLK_DEV, dtype=jnp.int32)) & slot_live[..., None]
    live_own = jnp.any(matches, axis=2).astype(f32)
    tiles = live_own.shape[1]

    enc_own, dec_own = enc_weight[0], dec_self[0]
    small_own = jnp.concatenate([norm_gain[0], enc_bias[0], live_own.reshape(-1)])
    enc_other = swapped(enc_own)
    dec_other = swapped(dec_own)
    small_other = swapped(small_own)

    def parts_of(values):
        gain = values[:cols]
        bias = values[cols : cols + width].reshape(1, width)
        live = values[cols + width :].reshape(batches, tiles, BLK_DEV)
        live = lax.dynamic_slice_in_dim(live, segment_index * half, half, 0)
        return gain, bias, jnp.repeat(live.astype(bf16), BLOCK, axis=2)

    gain0, bias0, live0 = parts_of(jnp.where(is_first, small_own, small_other))
    gain1, bias1, live1 = parts_of(jnp.where(is_first, small_other, small_own))
    live0 = jnp.broadcast_to(
        live0.transpose(1, 0, 2)[:, None, :, None, :], (tiles, dps // tiles, half, own_rows, width)
    ).reshape(rows, width)
    live1 = jnp.broadcast_to(
        live1[:, None, :, None, :], (half, latents // half, tiles, some // tiles, width)
    ).reshape(rows, width)

    mine = lax.dynamic_slice_in_dim(resid_in, segment_index * half, half, 0)
    by_dp = spread(mine.reshape(group, own_cols), "dp").reshape(rows, own_cols)
    resid0 = spread(by_dp, "latent")

    weights = [enc_own, enc_other, dec_own, dec_other]
    sems = pltpu.SemaphoreType.DMA((PIECES,))
    partial0, active0, held = call(
        functools.partial(first_layer, dps, pair),
        [array((latents, some, cols)), array((rows, width)), array((latents, some, own_cols))],
        [resid0, gain0.reshape(latents, own_cols), bias0, live0] + weights,
        hbm=4,
        scratch=[pltpu.VMEM(enc_own.shape, bf16), pltpu.VMEM(dec_own.shape, bf16), sems, sems],
        limit=32 * 1024 * 1024,
    )
    held = held.transpose(1, 0, 2).reshape(some, cols)
    down = 2
    block = (dps, some // down, cols * down // dps)
    share0 = call(sum_parts, array(block, f32), [exchanged(partial0, "latent")], limit=16 * 1024 * 1024)
    recon0 = call(sum_and_spread, array(block, f32), [exchanged(share0, "dp")])
    normed1, recon0 = call(
        add_and_normalize,
        [array((latents, some, cols)), array((some, cols))],
        [exchanged(recon0, "dp"), held, gain1.reshape(1, cols)],
        scratch=[pltpu.VMEM((some, cols), f32)],
        limit=16 * 1024 * 1024,
    )
    normed1 = exchanged(normed1, "latent")

    outgoing = call(
        functools.partial(second_layer, dps, pair),
        array((latents, rows + some, own_cols)),
        [normed1, active0, bias1, live1, recon0] + weights + [dec_cross],
        hbm=5,
        scratch=[pltpu.VMEM(enc_own.shape, bf16)] + [pltpu.VMEM(dec_own.shape, bf16)] * 2 + [sems] * 3,
        limit=40 * 1024 * 1024,
    )
    incoming = exchanged(outgoing, "latent")
    share1 = call(
        functools.partial(sum_for_dp, rows, dps, pair),
        array((2, dps, group, own_cols)),
        [incoming],
        limit=16 * 1024 * 1024,
    )
    final = exchanged(share1.reshape(2 * dps, group, own_cols), ("segment", "dp"))
    result = call(finish, array((2, group, own_cols)), [final.reshape(2, dps, group, own_cols)])
    return result.reshape(1, batches, own_rows, own_cols)


def solution(mesh):
    return jax.shard_map(
        body,
        mesh=mesh,
        in_specs=(
            P(None, "dp", "latent"),
            P("segment", None),
            P("segment", None, ("latent", "dp")),
            P("segment", ("latent", "dp")),
            P("segment", ("latent", "dp"), None),
            P(("latent", "dp"), None),
            P("segment", None, None, ("latent", "dp"), None),
            P("segment", None, None, ("latent", "dp")),
        ),
        out_specs=P("segment", None, "dp", "latent"),
        check_vma=False,
    )
```

time: 213 us -> 205 us (0.962); the launches traced: 210 us -> 205 us
  blocking collectives: 55.9 us -> 102 us
  waiting for transfers between devices: 88.4 us -> 56.7 us
  matrix products: 19.9 us -> 0 us
  Pallas kernels: 0 us -> 16.4 us
  starting transfers between devices: 25.7 us -> 16.3 us
  other arithmetic: 5.26 us -> 0.24 us
    all_to_all x3 -> x5, blocking collectives: 55.9 us -> 102 us  [exchanged(): return lax.all_to_all(value, axis, 0, 0)]
    all_to_all x5 -> x3, waiting for transfers between devices: 86.1 us -> 55.5 us  [exchanged(): return lax.all_to_all(value, axis, 0, 0)]
    dot_general x5 -> x0, matrix products: 19.9 us -> none  [the longest x2 8.88 us: encode(): jnp.dot(normed, enc[layer], preferred_element_type=jnp.float32) + bias]
    pallas_call x0 -> x7, Pallas kernels: none -> 16.4 us  [call(): pl.pallas_call(kernel, out_shape=outs, in_specs=[vmem] * (len(ins) - hbm)...]
    all_to_all x5 -> x3, starting transfers between devices: 25 us -> 15.7 us  [exchanged(): return lax.all_to_all(value, axis, 0, 0)]
    reshape x8 -> x4, local copies, waits for them, and re-layouts: 8.77 us -> 0.36 us  [the longest x1 0.18 us: body(): held = held.transpose(1, 0, 2).reshape(some, cols)]
    unnamed x19 -> x18, local copies, waits for them, and re-layouts: 1.38 us -> 7.66 us
    reduce_sum x6 -> x0, other arithmetic: 2.88 us -> none  [the longest x4 2.22 us: summed(): return jnp.sum(parts.astype(jnp.float32), axis=0).astype(jnp.bfloat16)]
  transfers between devices with their start and end apart: 9 -> 6, of which waited for: 7 -> 4; matrix products, arithmetic and copies ran while one was open for 8% -> 3% of each run, Pallas kernels for 0% -> 0%
where the time goes in v2:
time: 205 us
  blocking collectives  102 us (50%)
  waiting for transfers between devices  56.7 us (28%)
  Pallas kernels  16.4 us (8%)
  starting transfers between devices  16.3 us (8%)
  local copies, waits for them, and re-layouts  13 us (6%)
    all_to_all x5, blocking collectives, exchanged(): return lax.all_to_all(value, axis, 0, 0)  102 us
    all_to_all x3, waiting for transfers between devices, exchanged(): return lax.all_to_all(value, axis, 0, 0)  55.5 us
    pallas_call x7, Pallas kernels, call(): pl.pallas_call(kernel, out_shape=outs, in_specs=[vmem] * (len(ins) - hbm)...  16.4 us
    all_to_all x3, starting transfers between devices, exchanged(): return lax.all_to_all(value, axis, 0, 0)  15.7 us
    unnamed x18, local copies, waits for them, and re-layouts  7.66 us
  transfers between devices with their start and end apart: 6, of which 4 were waited for; matrix products, arithmetic and copies ran while one was open for 3% of the time, Pallas kernels for 0%

profile of v2, /device:TPU:32, one launch (start us, length us, event | category | flops | bytes accessed | tf_op | source)
XLA Modules:
  0.0 204.6 jit_solution(10650701631779005991)
XLA Ops:
  0.0 0.5 collective-permute-start.2
  0.8 15.8 %all_to_all.40 = bf16[8,32,224]{2,1,0:T(8,128)(2,1)S(1)} all-to-all(bf16[8,32,224]{2,1,0:T(8,128)(2,1)S(1)} %broadcast_in_dim.37), channel_id=1, replica_groups=mesh['segment'=2,'latent'=16,'dp'=8] {'dp'}, dimensions={0} | all-to-all | bytes 229376 | tf_op jit(solution)/shard_map/all_to_all | solution.py:25
  16.7 1.4 broadcast_in_dim.39
  18.1 7.2 %all-to-all-start.1 = ((bf16[16,256,224]{1,2,0:T(8,128)(2,1)}), bf16[16,256,224]{1,2,0:T(8,128)(2,1)}, u32[]{:S(2)}, u32[]{:S(2)}) async-start(bf16[16,256,224]{1,2,0:T(8,128)(2,1)} %broadcast_in_dim.39), calls=%async_computation.1 | async-start | bytes 3670016 | tf_op jit(solution)/shard_map/all_to_all | solution.py:25
  25.9 1.2 collective-permute-done
  27.6 23.5 %all-to-all-done.1 = bf16[16,256,224]{1,2,0:T(8,128)(2,1)} async-done(((bf16[16,256,224]{1,2,0:T(8,128)(2,1)}), bf16[16,256,224]{1,2,0:T(8,128)(2,1)}, u32[]{:S(2)}, u32[]{:S(2)}) %all-to-all-start.1) | async-done | bytes 1835040 | tf_op jit(solution)/shard_map/all_to_all | solution.py:25
  51.1 2.8 %copy.24.x_ref = bf16[16,256,224]{2,1,0:T(8,128)(2,1)S(1)} copy(bf16[16,256,224]{1,2,0:T(8,128)(2,1)} %all-to-all-done.1) | data formatting | bytes 3670016 | tf_op jit(solution)/shard_map/all_to_all | solution.py:25
  53.9 2.0 copy-done.1
  55.9 2.0 copy-done.3
  58.0 5.5 %shard_map.82 = (bf16[16,16,3584]{2,1,0:T(8,128)(2,1)S(1)}, bf16[256,512]{1,0:T(8,128)(2,1)S(1)}, bf16[16,16,224]{2,1,0:T(8,128)(2,1)S(1)}) custom-call(bf16[16,256,224]{2,1,0:T(8,128)(2,1)S(1)} %copy.24.x_ref, f32[16,224]{1,0:T(8,128)S(1)} %reshape.64.gain_ref, f32[1,512]{1,0:T(1,128)S(1)} %bitcast.33, bf16[256,512]{1,0:T(8,128)(2,1)S(1)} %bitcast.30, ...), custom_call_target="tpu_custom_call" | custom-call | tf_op jit(solution)/shard_map/pallas_call | solution.py:217
  63.4 28.0 %all_to_all.41.x_ref = bf16[16,16,3584]{2,1,0:T(8,128)(2,1)S(1)} all-to-all(bf16[16,16,3584]{2,1,0:T(8,128)(2,1)S(1)} %get-tuple-element.10), channel_id=1, replica_groups=mesh['segment'=2,'latent'=16,'dp'=8] {'latent'}, dimensions={0} | all-to-all | bytes 3670016 | tf_op jit(solution)/shard_map/all_to_all | solution.py:25
  91.7 13.0 %all_to_all.42.x_ref = f32[8,8,896]{2,1,0:T(8,128)} all-to-all(f32[8,8,896]{2,1,0:T(8,128)S(1)} %shard_map.83), channel_id=1, replica_groups=mesh['segment'=2,'latent'=16,'dp'=8] {'dp'}, dimensions={0} | all-to-all | bytes 458752 | tf_op jit(solution)/shard_map/all_to_all | solution.py:25
  104.7 1.7 shard_map.84
  106.4 4.8 %all-to-all-start.4 = ((f32[8,8,896]{2,1,0:T(8,128)}), f32[8,8,896]{2,1,0:T(8,128)S(1)}, u32[]{:S(2)}, u32[]{:S(2)}) async-start(f32[8,8,896]{2,1,0:T(8,128)} %shard_map.84), calls=%async_computation.4 | async-start | bytes 458752 | tf_op jit(solution)/shard_map/all_to_all | solution.py:25
  111.4 8.2 %all-to-all-done.4.pieces_ref = f32[8,8,896]{2,1,0:T(8,128)S(1)} async-done(((f32[8,8,896]{2,1,0:T(8,128)}), f32[8,8,896]{2,1,0:T(8,128)S(1)}, u32[]{:S(2)}, u32[]{:S(2)}) %all-to-all-start.4) | async-done | bytes 229408 | tf_op jit(solution)/shard_map/all_to_all | solution.py:25
  119.8 1.3 copy-done.4
  121.1 3.7 %all-to-all-start.5 = ((bf16[16,16,3584]{2,1,0:T(8,128)(2,1)}), bf16[16,16,3584]{2,1,0:T(8,128)(2,1)S(1)}, u32[]{:S(2)}, u32[]{:S(2)}) async-start(bf16[16,16,3584]{2,1,0:T(8,128)(2,1)} %copy-done.4), calls=%async_computation.5 | async-start | bytes 3670016 | tf_op jit(solution)/shard_map/all_to_all | solution.py:25
  125.0 23.8 %all-to-all-done.5.x_ref = bf16[16,16,3584]{2,1,0:T(8,128)(2,1)S(1)} async-done(((bf16[16,16,3584]{2,1,0:T(8,128)(2,1)}), bf16[16,16,3584]{2,1,0:T(8,128)(2,1)S(1)}, u32[]{:S(2)}, u32[]{:S(2)}) %all-to-all-start.5) | async-done | bytes 1835040 | tf_op jit(solution)/shard_map/all_to_all | solution.py:25
  148.9 2.0 copy-done.2
  150.9 6.8 %shard_map.86 = bf16[16,272,224]{2,1,0:T(8,128)(2,1)S(1)} custom-call(bf16[16,16,3584]{2,1,0:T(8,128)(2,1)S(1)} %all-to-all-done.5.x_ref, bf16[256,512]{1,0:T(8,128)(2,1)S(1)} %get-tuple-element.13.active_ref, f32[1,512]{1,0:T(1,128)S(1)} %bitcast.32, bf16[256,512]{1,0:T(8,128)(2,1)S(1)} %bitcast.28, bf16[16,3584]{1,0:T(8,128)(2,1)S(1)} %get-tuple-element.14.recon_ref, ...), custom_call_target="tpu_custom_call" | custom-call | tf_op jit(solution)/shard_map/pallas_call | solution.py:217
  157.7 29.1 %all_to_all.43.x_ref = bf16[16,272,224]{2,1,0:T(8,128)(2,1)S(1)} all-to-all(bf16[16,272,224]{2,1,0:T(8,128)(2,1)S(1)} %shard_map.86), channel_id=1, replica_groups=mesh['segment'=2,'latent'=16,'dp'=8] {'latent'}, dimensions={0} | all-to-all | bytes 3899392 | tf_op jit(solution)/shard_map/all_to_all | solution.py:25
  186.8 0.4 shard_map.87
  187.2 15.8 %all_to_all.44 = bf16[16,32,224]{2,1,0:T(8,128)(2,1)} all-to-all(bf16[16,32,224]{2,1,0:T(8,128)(2,1)S(1)} %bitcast.29), channel_id=1, replica_groups=mesh['segment'=2,'latent'=16,'dp'=8] {'segment','dp'}, dimensions={0} | all-to-all | bytes 458752 | tf_op jit(solution)/shard_map/all_to_all | solution.py:25
  203.0 1.6 shard_map.88
  (51 shorter events, 2.3 us)
Async XLA Ops:
  0.0 0.8 copy-start
  0.0 53.8 %collective-permute-start.1 = (bf16[3584,512]{1,0:T(8,128)(2,1)}, bf16[3584,512]{1,0:T(8,128)(2,1)}, u32[]{:S(2)}, u32[]{:S(2)}) collective-permute-start(bf16[3584,512]{1,0:T(8,128)(2,1)} %bitcast.22), channel_id=1, source_target_pairs={{0,128},{128,0},{1,129},{129,1},{2,130},{130,2},{3,131},{131,3},{4... | collective-permute-start | bytes 11010056 | tf_op jit(solution)/shard_map/ppermute | solution.py:21
  0.0 53.9 %collective-permute-start.2 = (bf16[512,3584]{1,0:T(8,128)(2,1)}, bf16[512,3584]{1,0:T(8,128)(2,1)}, u32[]{:S(2)}, u32[]{:S(2)}) collective-permute-start(bf16[512,3584]{1,0:T(8,128)(2,1)} %bitcast.25), channel_id=1, source_target_pairs={{0,128},{128,0},{1,129},{129,1},{2,130},{130,2},{3,131},{131,3},{4... | collective-permute-start | bytes 11010056 | tf_op jit(solution)/shard_map/ppermute | solution.py:21
  18.1 7.2 %copy-start.8 = (s32[1,4,2,1]{1,3,2,0:T(1,128)S(1)}, s32[1,4,2,1]{1,3,2,0:T(1,128)}, u32[]{:S(2)}) copy-start(s32[1,4,2,1]{1,3,2,0:T(1,128)} %param.15) | copy-start | bytes 100
  18.1 7.4 %copy-start.7 = (s32[1,4,2,1,4]{4,3,2,1,0:T(1,128)S(1)}, s32[1,4,2,1,4]{4,3,2,1,0:T(1,128)}, u32[]{:S(2)}) copy-start(s32[1,4,2,1,4]{4,3,2,1,0:T(1,128)} %param.14) | copy-start | bytes 388
  18.1 7.6 %copy-start.5 = (f32[1,3584]{1,0:T(1,128)S(1)}, f32[1,3584]{1,0:T(1,128)}, u32[]{:S(2)}) copy-start(f32[1,3584]{1,0:T(1,128)} %param.9) | copy-start | bytes 43012
  18.1 7.7 %copy-start.6 = (f32[1,512]{1,0:T(1,128)S(1)}, f32[1,512]{1,0:T(1,128)}, u32[]{:S(2)}) copy-start(f32[1,512]{1,0:T(1,128)} %param.11) | copy-start | bytes 6148
  18.1 32.9 %all-to-all-start.1 = ((bf16[16,256,224]{1,2,0:T(8,128)(2,1)}), bf16[16,256,224]{1,2,0:T(8,128)(2,1)}, u32[]{:S(2)}, u32[]{:S(2)}) async-start(bf16[16,256,224]{1,2,0:T(8,128)(2,1)} %broadcast_in_dim.39), calls=%async_computation.1 | async-start | bytes 3670016 | tf_op jit(solution)/shard_map/all_to_all | solution.py:25
  25.8 1.3 collective-permute-start
  53.9 2.0 copy-start.1
  55.9 2.0 copy-start.3
  106.4 13.2 %all-to-all-start.4 = ((f32[8,8,896]{2,1,0:T(8,128)}), f32[8,8,896]{2,1,0:T(8,128)S(1)}, u32[]{:S(2)}, u32[]{:S(2)}) async-start(f32[8,8,896]{2,1,0:T(8,128)} %shard_map.84), calls=%async_computation.4 | async-start | bytes 458752 | tf_op jit(solution)/shard_map/all_to_all | solution.py:25
  119.8 1.3 copy-start.4
  121.1 27.7 %all-to-all-start.5 = ((bf16[16,16,3584]{2,1,0:T(8,128)(2,1)}), bf16[16,16,3584]{2,1,0:T(8,128)(2,1)S(1)}, u32[]{:S(2)}, u32[]{:S(2)}) async-start(bf16[16,16,3584]{2,1,0:T(8,128)(2,1)} %copy-done.4), calls=%async_computation.5 | async-start | bytes 3670016 | tf_op jit(solution)/shard_map/all_to_all | solution.py:25
  148.9 2.0 copy-start.2

commit v3 on v2

v3 whole, which is shorter than its diff:
```python
import functools

import jax
import jax.numpy as jnp
from jax import lax
from jax.experimental import pallas as pl
from jax.experimental.pallas import tpu as pltpu
from jax.sharding import PartitionSpec as P

BLK_DEV = 8
BLOCK = 64
PIECES = 4

norm_eps = 1e-06

f32 = jnp.float32
bf16 = jnp.bfloat16


def swapped(value):
    return lax.ppermute(value, "segment", [(0, 1), (1, 0)])


def exchanged(value, axis):
    return lax.all_to_all(value, axis, 0, 0)


def one_hot(shape, column_of_row):
    row = lax.broadcasted_iota(jnp.int32, shape, 0)
    column = lax.broadcasted_iota(jnp.int32, shape, 1)
    return (column == column_of_row(row)).astype(f32).astype(bf16)


def dot(left, right):
    return jnp.dot(left, right, preferred_element_type=f32)


def copies(source, target, sems, axis):
    size = target.shape[axis] // PIECES
    made = []
    for piece in range(PIECES):
        part = pl.ds(piece * size, size)
        index = (part, slice(None)) if axis == 0 else (slice(None), part)
        made.append(pltpu.make_async_copy(source.at[index], target.at[index], sems.at[piece]))
    return made


def start_from(choose_first, first, second, target, sems, axis):
    @pl.when(choose_first)
    def _():
        for copy in copies(first, target, sems, axis):
            copy.start()

    @pl.when(jnp.logical_not(choose_first))
    def _():
        for copy in copies(second, target, sems, axis):
            copy.start()

    return copies(first, target, sems, axis)


def live_row(list_ref, batch, tile, width):
    block = lax.broadcasted_iota(jnp.int32, (1, width), 1) // BLOCK
    live = jnp.zeros((1, width), f32)
    for slot in range(list_ref.shape[4]):
        live = jnp.where(block == list_ref[0, batch, tile, 0, slot], 1.0, live)
    return live


def live_rows(choose_first, first, second, batch, tile, count, width):
    row = jnp.where(
        choose_first, live_row(first, batch, tile, width), live_row(second, batch, tile, width)
    )
    return jnp.broadcast_to(row, (count, width))


def first_layer(latents, dps, x_ref, gain_own, gain_other, bias_own, bias_other, list_own, list_other,
                enc_own, enc_other, dec_own, dec_other,
                part_hbm, active_ref, held_ref, enc, dec, share, enc_sems, dec_sems, share_sems):
    group = x_ref.shape[1]
    rows = dps * group
    pair = group // latents
    cols = gain_own.shape[1]
    own_cols = cols // latents
    width = enc.shape[1]
    half, tiles = list_own.shape[1] // 2, list_own.shape[2]
    segment = lax.axis_index("segment")
    is_first = segment == 0
    latent = lax.axis_index("latent")
    enc_copies = start_from(is_first, enc_own, enc_other, enc, enc_sems, 0)
    gain = jnp.where(is_first, gain_own[...], gain_other[...])
    bias = jnp.where(is_first, bias_own[...], bias_other[...])
    step_latent = jnp.where(is_first, dps, 1)
    step_dp = jnp.where(is_first, 1, latents)

    def block(piece):
        parts = [x_ref[piece * step_latent + dp * step_dp] for dp in range(dps)]
        return jnp.concatenate(parts, axis=0)[:, :own_cols]

    squares = jnp.zeros((rows, own_cols), f32)
    for piece in range(latents):
        values = block(piece).astype(f32)
        squares += values * values
    scaling = lax.rsqrt(jnp.sum(squares, axis=1, keepdims=True) / cols + norm_eps)

    choose_own = one_hot(
        (dps * pair, rows), lambda row: (row // pair) * group + latent * pair + row % pair
    )
    total = jnp.zeros((rows, width), f32)
    dec_copies = []
    for piece in range(latents):
        if piece % (latents // PIECES) == 0:
            enc_copies[piece // (latents // PIECES)].wait()
            if piece == 0:
                dec_copies = start_from(is_first, dec_own, dec_other, dec, dec_sems, 1)
        own_gain = gain[:, piece * own_cols : (piece + 1) * own_cols]
        values = block(piece)
        held_ref[piece] = dot(choose_own, values).astype(bf16)
        normed = (values.astype(f32) * scaling * own_gain).astype(bf16)
        total += dot(normed, enc[pl.ds(piece * own_cols, own_cols), :])
    live = []
    for tile in range(tiles):
        some = [
            live_rows(is_first, list_own, list_other, segment * half + batch, tile, group // half, width)
            for batch in range(half)
        ]
        live += some * (dps // tiles)
    active = (jnp.maximum(total + bias, 0.0) * jnp.concatenate(live, axis=0)).astype(bf16)
    active_ref[...] = active
    to_owner = one_hot(
        (rows, rows),
        lambda row: ((row // pair) % dps) * group + row // (dps * pair) * pair + row % pair,
    )
    sorted_active = dot(to_owner, active).astype(bf16)
    size = cols // PIECES
    share_copies = []
    for piece in range(PIECES):
        dec_copies[piece].wait()
        part = pl.ds(piece * size, size)
        share[:, :, part] = dot(sorted_active, dec[:, part]).astype(bf16).reshape(latents, rows // latents, size)
        where = (slice(None), slice(None), part)
        copy = pltpu.make_async_copy(share.at[where], part_hbm.at[where], share_sems.at[piece])
        copy.start()
        share_copies.append(copy)
    for copy in share_copies:
        copy.wait()


def cut_decoder(own_segment, *refs):
    *_, dec_hbm, dec_out, dec, dec_part, dec_sems, out_sem = refs
    latents, _, own_cols = dec_out.shape
    size = dec.shape[1] // PIECES
    per_piece = latents // PIECES

    @pl.when(lax.axis_index("segment") == own_segment)
    def _():
        dec_copies = copies(dec_hbm, dec, dec_sems, 1)
        for copy in dec_copies:
            copy.start()
        for piece in range(PIECES):
            dec_copies[piece].wait()
            decoder = dec[:, pl.ds(piece * size, size)].astype(f32)
            for inner in range(per_piece):
                where = slice(inner * own_cols, (inner + 1) * own_cols)
                dec_part[piece * per_piece + inner] = decoder[:, where].astype(bf16)
        copy = pltpu.make_async_copy(dec_part, dec_out, out_sem)
        copy.start()
        copy.wait()


def cross_share(active_ref, cross_hbm, cross_out, cross, cross_part, cross_sems, out_sem):
    latents, _, own_cols = cross_out.shape
    cross_copies = copies(cross_hbm, cross, cross_sems, 1)
    for copy in cross_copies:
        copy.start()
    size = cross.shape[1] // PIECES
    per_piece = latents // PIECES
    earlier = active_ref[...]
    for piece in range(PIECES):
        cross_copies[piece].wait()
        share = dot(earlier, cross[:, pl.ds(piece * size, size)])
        for inner in range(per_piece):
            where = slice(inner * own_cols, (inner + 1) * own_cols)
            cross_part[piece * per_piece + inner] = share[:, where]
    copy = pltpu.make_async_copy(cross_part, cross_out, out_sem)
    copy.start()
    copy.wait()


def second_layer(dps, x_ref, recon_ref, bias_own, bias_other, list_own, list_other,
                 enc_own, enc_other, dec_hbm, cross_hbm, out_ref, enc, dec, cross, enc_sems, dec_sems, cross_sems):
    latents, some, cols = x_ref.shape
    rows = cross.shape[1]
    pair = some // dps
    group = rows // dps
    width = enc.shape[1]
    enc_copies = start_from(lax.axis_index("segment") == 0, enc_other, enc_own, enc, enc_sems, 0)
    dec_copies = copies(dec_hbm, dec, dec_sems, 0)
    cross_copies = copies(cross_hbm, cross, cross_sems, 0)
    half, tiles = list_own.shape[1] // 2, list_own.shape[2]
    segment = lax.axis_index("segment")
    is_first = segment == 0
    bias = jnp.where(is_first, bias_other[...], bias_own[...])
    size = cols // PIECES
    total = jnp.zeros((rows, width), f32)
    for piece in range(PIECES):
        enc_copies[piece].wait()
        dec_copies[piece].start()
        cross_copies[piece].start()
        part = pl.ds(piece * size, size)
        total += dot(x_ref[:, :, part].reshape(rows, size), enc[part, :])
    live = []
    for batch in range(half):
        both = [
            live_rows(is_first, list_other, list_own, segment * half + batch, tile, some // tiles, width)
            for tile in range(tiles)
        ]
        live += both * (latents // half)
    active = (jnp.maximum(total + bias, 0.0) * jnp.concatenate(live, axis=0)).astype(bf16)
    to_natural = one_hot(
        (rows, rows),
        lambda row: (row % group) // pair * some + row // group * pair + row % pair,
    )
    sorted_active = dot(to_natural, active).astype(bf16)
    for piece in range(latents):
        if piece % (latents // PIECES) == 0:
            dec_copies[piece // (latents // PIECES)].wait()
            cross_copies[piece // (latents // PIECES)].wait()
        out_ref[piece, pl.ds(0, rows), :] = (dot(sorted_active, dec[piece]) + cross[piece]).astype(bf16)
        out_ref[piece, pl.ds(rows, some), :] = recon_ref[piece]


def take_own(x_ref, out_ref):
    count, group, padded = out_ref.shape
    half = x_ref.shape[0] // 2
    own_cols = x_ref.shape[2]
    segment = lax.axis_index("segment")
    for batch in range(half):
        mine = x_ref[segment * half + batch].astype(f32)
        mine = jnp.concatenate([mine, jnp.zeros((mine.shape[0], padded - own_cols), f32)], axis=1).astype(bf16)
        for piece in range(count):
            out_ref[piece, pl.ds(batch * mine.shape[0], mine.shape[0]), :] = mine


def repeat(x_ref, out_ref):
    for piece in range(out_ref.shape[0]):
        out_ref[piece] = x_ref[...]


def sum_parts(x_ref, out_ref):
    total = x_ref[0].astype(f32)
    for source in range(1, x_ref.shape[0]):
        total += x_ref[source].astype(f32)
    _, height, width = out_ref.shape
    per_row = total.shape[1] // width
    for piece in range(out_ref.shape[0]):
        down, across = divmod(piece, per_row)
        out_ref[piece] = total[down * height : (down + 1) * height, across * width : (across + 1) * width]


def sum_and_spread(x_ref, out_ref):
    total = x_ref[0]
    for source in range(1, x_ref.shape[0]):
        total += x_ref[source]
    rounded = total.astype(bf16).astype(f32)
    for piece in range(out_ref.shape[0]):
        out_ref[piece] = rounded


def add_and_normalize(pieces_ref, held_ref, gain_own, gain_other, out_ref, recon_ref, wide):
    count, height, width = pieces_ref.shape
    cols = wide.shape[1]
    per_row = cols // width
    for piece in range(count):
        down, across = divmod(piece, per_row)
        wide[pl.ds(down * height, height), pl.ds(across * width, width)] = pieces_ref[piece]
    recon = wide[...]
    own_cols = recon_ref.shape[2]
    for piece in range(recon_ref.shape[0]):
        recon_ref[piece] = recon[:, piece * own_cols : (piece + 1) * own_cols].astype(bf16)
    resid = (held_ref[...].astype(f32) + recon).astype(bf16).astype(f32)
    scaling = lax.rsqrt(jnp.mean(resid * resid, axis=1, keepdims=True) + norm_eps)
    gain = jnp.where(lax.axis_index("segment") == 0, gain_other[...], gain_own[...])
    normed = (resid * scaling * gain).astype(bf16)
    for piece in range(out_ref.shape[0]):
        out_ref[piece] = normed


def sum_for_dp(rows, dps, pair, x_ref, out_ref):
    latents, taken, own_cols = x_ref.shape
    total = x_ref[0, pl.ds(0, rows), :].astype(f32)
    for source in range(1, latents):
        total += x_ref[source, pl.ds(0, rows), :].astype(f32)
    out_ref[1] = total.astype(bf16).reshape(dps, rows // dps, own_cols)
    extra = taken - rows
    dp = lax.axis_index("dp")
    choose_own = one_hot(
        (latents * pair, latents * extra),
        lambda row: (row // pair) * extra + dp * pair + row % pair,
    )
    recon = x_ref[:, pl.ds(rows, extra), :].reshape(latents * extra, own_cols)
    recon = dot(choose_own, recon).astype(bf16)
    for piece in range(dps):
        out_ref[0, piece] = recon


def finish(x_ref, out_ref):
    halves, dps = x_ref.shape[:2]
    is_first = lax.axis_index("segment") == 0
    dp = lax.axis_index("dp")
    for half in range(halves):
        total = x_ref[half, 0].astype(f32)
        for source in range(1, dps):
            total += x_ref[half, source].astype(f32)
        kept = x_ref[half, dp].astype(f32)
        out_ref[half] = jnp.where(is_first, kept, total).astype(bf16)


def call(kernel, outs, ins, scalars=0, hbm=0, scratch=(), limit=16, hbm_outs=0, aliases=None):
    vmem, far = pl.BlockSpec(memory_space=pltpu.VMEM), pl.BlockSpec(memory_space=pltpu.HBM)
    single = not isinstance(outs, (list, tuple))
    specs = [vmem] * (len(ins) - scalars - hbm)
    specs += [pl.BlockSpec(memory_space=pltpu.SMEM)] * scalars
    specs += [far] * hbm
    return pl.pallas_call(
        kernel,
        out_shape=outs,
        in_specs=specs,
        out_specs=vmem if single else [far] * hbm_outs + [vmem] * (len(outs) - hbm_outs),
        scratch_shapes=list(scratch),
        input_output_aliases=aliases or {},
        compiler_params=pltpu.CompilerParams(vmem_limit_bytes=limit * 1024 * 1024),
    )(*[placed(value, index, len(ins), hbm) for index, value in enumerate(ins)])


def placed(value, index, count, hbm):
    return pltpu.with_memory_space_constraint(value, pltpu.HBM) if index >= count - hbm else value


def array(shape, dtype=bf16, space=None):
    return jax.ShapeDtypeStruct(shape, dtype) if space is None else space(shape, dtype)


def body(resid_in, norm_gain, enc_weight, enc_bias, dec_self, dec_cross, block_ids, block_counts):
    is_first = lax.axis_index("segment") == 0
    latents = lax.axis_size("latent")
    dps = lax.axis_size("dp")
    batches, own_rows, own_cols = resid_in.shape
    cols = latents * own_cols
    width = enc_weight.shape[2]
    group = batches // 2 * own_rows
    some = dps * group // latents
    rows = group * dps
    padded = own_cols + -own_cols % 128

    enc_own, dec_own = enc_weight[0], dec_self[0]
    weights = [enc_own, swapped(enc_own), dec_own, swapped(dec_own)]
    gains = [norm_gain, swapped(norm_gain)]
    biases = [enc_bias, swapped(enc_bias)]
    slot = lax.broadcasted_iota(jnp.int32, block_ids.shape, block_ids.ndim - 1)
    listed = jnp.where(slot < block_counts[..., None], block_ids, -1)
    lists = [listed, swapped(listed)]

    def dp_first(resid):
        mine = call(take_own, array((dps, group, padded)), [resid])
        some_rows = exchanged(mine, "dp").reshape(rows, padded)
        every = call(repeat, array((latents, rows, padded)), [some_rows])
        return exchanged(every, "latent").reshape(latents * dps, group, padded)

    def latent_first(resid):
        mine = call(take_own, array((latents, group, padded)), [resid])
        some_cols = exchanged(mine, "latent").reshape(latents * group, padded)
        every = call(repeat, array((dps, latents * group, padded)), [some_cols])
        return exchanged(every, "dp").reshape(latents * dps, group, padded)

    resid0 = lax.cond(is_first, dp_first, latent_first, resid_in)

    sems = pltpu.SemaphoreType.DMA((PIECES,))
    enc_space, dec_space = pltpu.VMEM(enc_own.shape, bf16), pltpu.VMEM(dec_own.shape, bf16)
    partial0, active0, held = call(
        functools.partial(first_layer, latents, dps),
        [array((latents, some, cols), space=pltpu.HBM), array((rows, width)), array((latents, some, own_cols))],
        [resid0] + gains + biases + lists + weights,
        scalars=2,
        hbm=4,
        scratch=[enc_space, dec_space, pltpu.VMEM((latents, some, cols), bf16)] + [sems] * 3,
        limit=26,
        hbm_outs=1,
    )
    held = held.transpose(1, 0, 2).reshape(some, cols)
    dec_parts = pltpu.VMEM((latents, width, own_cols), bf16)
    cross_parts = pltpu.VMEM((latents, rows, own_cols), f32)
    one_sem = pltpu.SemaphoreType.DMA(())
    dec_cut = array((latents, width, own_cols), space=pltpu.HBM)
    cut_space = dict(scratch=[dec_space, dec_parts, sems, one_sem], limit=24, hbm_outs=1)
    dec1 = call(functools.partial(cut_decoder, 1), [dec_cut], [dec_own], hbm=1, **cut_space)[0]
    partial0, dec1 = lax.optimization_barrier((partial0, dec1))
    dec1 = call(
        functools.partial(cut_decoder, 0), [dec_cut], [dec1, weights[3]], hbm=2, aliases={0: 0}, **cut_space
    )[0]
    cross0 = call(
        cross_share,
        [array((latents, rows, own_cols), f32, space=pltpu.HBM)],
        [active0, dec_cross],
        hbm=1,
        scratch=[dec_space, cross_parts, sems, one_sem],
        limit=24,
        hbm_outs=1,
    )[0]
    down = 2
    block = (dps, some // down, cols * down // dps)
    arrived = exchanged(partial0, "latent")
    arrived, held, dec1, cross0 = lax.optimization_barrier((arrived, held, dec1, cross0))
    share0 = call(sum_parts, array(block, f32), [arrived])
    recon0 = call(sum_and_spread, array(block, f32), [exchanged(share0, "dp")])
    normed1, recon0 = call(
        add_and_normalize,
        [array((latents, some, cols)), array((latents, some, own_cols))],
        [exchanged(recon0, "dp"), held] + gains,
        scratch=[pltpu.VMEM((some, cols), f32)],
    )
    normed1 = exchanged(normed1, "latent")

    outgoing = call(
        functools.partial(second_layer, dps),
        array((latents, rows + some, own_cols)),
        [normed1, recon0] + biases + lists + weights[:2] + [dec1, cross0],
        scalars=2,
        hbm=4,
        scratch=[enc_space, dec_parts, cross_parts] + [sems] * 3,
        limit=32,
    )
    incoming = exchanged(outgoing, "latent")
    share1 = call(
        functools.partial(sum_for_dp, rows, dps, some // dps),
        array((2, dps, group, own_cols)),
        [incoming],
    )
    final = exchanged(share1.reshape(2 * dps, group, own_cols), ("segment", "dp"))
    result = call(finish, array((2, group, own_cols)), [final.reshape(2, dps, group, own_cols)])
    return result.reshape(1, batches, own_rows, own_cols)


def solution(mesh):
    return jax.shard_map(
        body,
        mesh=mesh,
        in_specs=(
            P(None, "dp", "latent"),
            P("segment", None),
            P("segment", None, ("latent", "dp")),
            P("segment", ("latent", "dp")),
            P("segment", ("latent", "dp"), None),
            P(("latent", "dp"), None),
            P("segment", None, None, ("latent", "dp"), None),
            P("segment", None, None, ("latent", "dp")),
        ),
        out_specs=P("segment", None, "dp", "latent"),
        check_vma=False,
    )
```

time: 205 us -> 185 us (0.902)
  waiting for transfers between devices: 56.7 us -> 9.25 us
  blocking collectives: 102 us -> 140 us
  starting transfers between devices: 16.3 us -> 4.82 us
  local copies, waits for them, and re-layouts: 13 us -> 2.97 us
  Pallas kernels: 16.4 us -> 26.1 us
    all_to_all x3 -> x1, waiting for transfers between devices: 55.5 us -> 9.24 us  [exchanged(): return lax.all_to_all(value, axis, 0, 0)]
    all_to_all x5 -> x7, blocking collectives: 102 us -> 140 us  [exchanged(): return lax.all_to_all(value, axis, 0, 0)]
    all_to_all x3 -> x1, starting transfers between devices: 15.7 us -> 3.72 us  [exchanged(): return lax.all_to_all(value, axis, 0, 0)]
    pallas_call x7 -> x12, Pallas kernels: 16.4 us -> 26.1 us  [call(): pl.pallas_call(kernel, out_shape=outs, in_specs=specs, out_specs=vmem if...]
    unnamed x18 -> x8, local copies, waits for them, and re-layouts: 7.66 us -> 1.99 us
    all_to_all x1 -> x0, local copies, waits for them, and re-layouts: 2.79 us -> none  [exchanged(): return lax.all_to_all(value, axis, 0, 0)]
  transfers between devices with their start and end apart: 6 -> 6, of which waited for: 4 -> 1; matrix products, arithmetic and copies ran while one was open for 3% -> 1% of each run, Pallas kernels for 0% -> 6%
where the time goes in v3:
time: 185 us
  blocking collectives  140 us (76%)
  Pallas kernels  26.1 us (14%)
  waiting for transfers between devices  9.25 us (5%)
  starting transfers between devices  4.82 us (3%)
  local copies, waits for them, and re-layouts  2.97 us (2%)
    all_to_all x7, blocking collectives, exchanged(): return lax.all_to_all(value, axis, 0, 0)  140 us
    pallas_call x12, Pallas kernels, call(): pl.pallas_call(kernel, out_shape=outs, in_specs=specs, out_specs=vmem if...  26.1 us
    all_to_all x1, waiting for transfers between devices, exchanged(): return lax.all_to_all(value, axis, 0, 0)  9.24 us
    all_to_all x1, starting transfers between devices, exchanged(): return lax.all_to_all(value, axis, 0, 0)  3.72 us
  transfers between devices with their start and end apart: 6, of which 1 were waited for; matrix products, arithmetic and copies ran while one was open for 1% of the time, Pallas kernels for 6%

profile of v3, /device:TPU:32, one launch (start us, length us, event | category | flops | bytes accessed | tf_op | source)
XLA Modules:
  0.0 184.5 jit_solution(13503444170831362192)
XLA Ops:
  0.0 0.5 collective-permute-start.4
  0.5 0.5 collective-permute-start.1
  1.0 0.8 copy.10
  1.8 0.8 compare_select_fusion.list_own
  2.7 0.7 copy-done.3
  3.4 41.7 %conditional.1 = (bf16[128,32,256]{2,1,0:T(8,128)(2,1)S(1)}) conditional(s32[]{:T(128)} %convert_element_type.3, bf16[4,16,224]{2,1,0:T(8,128)(2,1)S(1)} %copy-done.3, bf16[4,16,224]{2,1,0:T(8,128)(2,1)S(1)} %copy-done.3), branch_computations={%region_0.1_spmd, %region_1.2_spmd} | conditional | bytes 4718600 | solution.py:376
  3.4 16.0 %all_to_all.48 = bf16[8,32,256]{2,1,0:T(8,128)(2,1)S(1)} all-to-all(bf16[8,32,256]{2,1,0:T(8,128)(2,1)S(1)} %branch_1_fun.2), channel_id=1, replica_groups=mesh['segment'=2,'latent'=16,'dp'=8] {'dp'}, dimensions={0} | all-to-all | bytes 262144 | tf_op jit(solution)/shard_map/cond/branch_1_fun/all_to_all | solution.py:25
  19.5 25.5 %all_to_all.49 = bf16[16,256,256]{2,1,0:T(8,128)(2,1)S(1)} all-to-all(bf16[16,256,256]{2,1,0:T(8,128)(2,1)S(1)} %branch_1_fun.3), channel_id=1, replica_groups=mesh['segment'=2,'latent'=16,'dp'=8] {'latent'}, dimensions={0} | all-to-all | bytes 4194304 | tf_op jit(solution)/shard_map/cond/branch_1_fun/all_to_all | solution.py:25
  45.1 1.3 copy-done.2
  46.4 7.8 %shard_map.88 = (bf16[16,16,3584]{2,1,0:T(8,128)(2,1)}, bf16[256,512]{1,0:T(8,128)(2,1)S(1)}, bf16[16,16,224]{2,1,0:T(8,128)(2,1)S(1)}) custom-call(bf16[128,32,256]{2,1,0:T(8,128)(2,1)} %copy-done.2, f32[1,3584]{1,0:T(1,128)S(1)} %copy-done, f32[1,3584]{1,0:T(1,128)S(1)} %collective-permute-done.gain_other, f32[1,512]{1,0:T(1,128)S(1)} %copy-done.1, ...), custom_call_target="tpu_custom_call" | custom-call | tf_op jit(solution)/shard_map/pallas_call | solution.py:325
  54.2 3.7 %all-to-all-start.4 = ((bf16[16,16,3584]{2,1,0:T(8,128)(2,1)}), bf16[16,16,3584]{2,1,0:T(8,128)(2,1)S(1)}, u32[]{:S(2)}, u32[]{:S(2)}) async-start(bf16[16,16,3584]{2,1,0:T(8,128)(2,1)} %get-tuple-element.22), calls=%async_computation.4 | async-start | bytes 3670016 | tf_op jit(solution)/shard_map/all_to_all | solution.py:25
  58.2 5.5 %shard_map.91.cross_hbm = f32[16,256,224]{2,1,0:T(8,128)} custom-call(bf16[256,512]{1,0:T(8,128)(2,1)S(1)} %get-tuple-element.25.active_ref, bf16[512,3584]{1,0:T(8,128)(2,1)} %cross_hbm.1), custom_call_target="tpu_custom_call" | custom-call | tf_op jit(solution)/shard_map/pallas_call | solution.py:325
  63.7 5.0 %shard_map.90.dec_hbm = bf16[16,512,224]{2,1,0:T(8,128)(2,1)} custom-call(bf16[16,512,224]{2,1,0:T(8,128)(2,1)} %shard_map.89.refs_0_, bf16[512,3584]{1,0:T(8,128)(2,1)} %collective-permute-done.4.dec_other.refs_1_), custom_call_target="tpu_custom_call", output_to_operand_aliasing={{}: (0, {})} | custom-call | tf_op jit(solution)/shard_map/pallas_call | solution.py:325
  68.7 9.2 %all-to-all-done.4.x_ref = bf16[16,16,3584]{2,1,0:T(8,128)(2,1)S(1)} async-done(((bf16[16,16,3584]{2,1,0:T(8,128)(2,1)}), bf16[16,16,3584]{2,1,0:T(8,128)(2,1)S(1)}, u32[]{:S(2)}, u32[]{:S(2)}) %all-to-all-start.4) | async-done | bytes 1835040 | tf_op jit(solution)/shard_map/all_to_all | solution.py:25
  77.9 0.2 shard_map.92
  78.2 12.3 %all_to_all.50.x_ref = f32[8,8,896]{2,1,0:T(8,128)S(1)} all-to-all(f32[8,8,896]{2,1,0:T(8,128)S(1)} %shard_map.92), channel_id=1, replica_groups=mesh['segment'=2,'latent'=16,'dp'=8] {'dp'}, dimensions={0} | all-to-all | bytes 458752 | tf_op jit(solution)/shard_map/all_to_all | solution.py:25
  90.5 12.8 %all_to_all.51.pieces_ref = f32[8,8,896]{2,1,0:T(8,128)S(1)} all-to-all(f32[8,8,896]{2,1,0:T(8,128)S(1)} %shard_map.93), channel_id=1, replica_groups=mesh['segment'=2,'latent'=16,'dp'=8] {'dp'}, dimensions={0} | all-to-all | bytes 458752 | tf_op jit(solution)/shard_map/all_to_all | solution.py:25
  103.3 0.3 shard_map.94
  103.6 26.3 %all_to_all.52.x_ref = bf16[16,16,3584]{2,1,0:T(8,128)(2,1)S(1)} all-to-all(bf16[16,16,3584]{2,1,0:T(8,128)(2,1)S(1)} %get-tuple-element.28), channel_id=1, replica_groups=mesh['segment'=2,'latent'=16,'dp'=8] {'latent'}, dimensions={0} | all-to-all | bytes 3670016 | tf_op jit(solution)/shard_map/all_to_all | solution.py:25
  129.9 6.0 %shard_map.95 = bf16[16,272,224]{2,1,0:T(8,128)(2,1)S(1)} custom-call(bf16[16,16,3584]{2,1,0:T(8,128)(2,1)S(1)} %all_to_all.52.x_ref, bf16[16,16,224]{2,1,0:T(8,128)(2,1)S(1)} %get-tuple-element.29.recon_ref, f32[1,512]{1,0:T(1,128)S(1)} %copy-done.1, f32[1,512]{1,0:T(1,128)S(1)} %collective-permute-done.1.bias_other, ...), custom_call_target="tpu_custom_call" | custom-call | tf_op jit(solution)/shard_map/pallas_call | solution.py:325
  135.9 29.3 %all_to_all.53.x_ref = bf16[16,272,224]{2,1,0:T(8,128)(2,1)S(1)} all-to-all(bf16[16,272,224]{2,1,0:T(8,128)(2,1)S(1)} %shard_map.95), channel_id=1, replica_groups=mesh['segment'=2,'latent'=16,'dp'=8] {'latent'}, dimensions={0} | all-to-all | bytes 3899392 | tf_op jit(solution)/shard_map/all_to_all | solution.py:25
  165.2 0.4 shard_map.96
  165.6 18.2 %all_to_all.54 = bf16[16,32,224]{2,1,0:T(8,128)(2,1)S(1)} all-to-all(bf16[16,32,224]{2,1,0:T(8,128)(2,1)S(1)} %bitcast.12), channel_id=1, replica_groups=mesh['segment'=2,'latent'=16,'dp'=8] {'segment','dp'}, dimensions={0} | all-to-all | bytes 458752 | tf_op jit(solution)/shard_map/all_to_all | solution.py:25
  183.8 0.7 shard_map.97
  (20 shorter events, 0.6 us)
Async XLA Ops:
  0.0 45.1 %collective-permute-start.3 = (bf16[3584,512]{1,0:T(8,128)(2,1)}, bf16[3584,512]{1,0:T(8,128)(2,1)}, u32[]{:S(2)}, u32[]{:S(2)}) collective-permute-start(bf16[3584,512]{1,0:T(8,128)(2,1)} %bitcast.16), channel_id=1, source_target_pairs={{0,128},{128,0},{1,129},{129,1},{2,130},{130,2},{3,131},{131,3},{4... | collective-permute-start | bytes 11010056 | tf_op jit(solution)/shard_map/ppermute | solution.py:21
  0.0 46.4 %collective-permute-start.4 = (bf16[512,3584]{1,0:T(8,128)(2,1)}, bf16[512,3584]{1,0:T(8,128)(2,1)}, u32[]{:S(2)}, u32[]{:S(2)}) collective-permute-start(bf16[512,3584]{1,0:T(8,128)(2,1)} %bitcast.19), channel_id=1, source_target_pairs={{0,128},{128,0},{1,129},{129,1},{2,130},{130,2},{3,131},{131,3},{4... | collective-permute-start | bytes 11010056 | tf_op jit(solution)/shard_map/ppermute | solution.py:21
  0.5 44.6 %collective-permute-start = (f32[1,3584]{1,0:T(1,128)}, f32[1,3584]{1,0:T(1,128)S(1)}, u32[]{:S(2)}, u32[]{:S(2)}) collective-permute-start(f32[1,3584]{1,0:T(1,128)} %gain_own.3), channel_id=1, source_target_pairs={{0,128},{128,0},{1,129},{129,1},{2,130},{130,2},{3,131},{131,3},{4... | collective-permute-start | bytes 43016 | tf_op jit(solution)/shard_map/ppermute | solution.py:21
  0.5 44.6 %collective-permute-start.1 = (f32[1,512]{1,0:T(1,128)}, f32[1,512]{1,0:T(1,128)S(1)}, u32[]{:S(2)}, u32[]{:S(2)}) collective-permute-start(f32[1,512]{1,0:T(1,128)} %bias_own.3), channel_id=1, source_target_pairs={{0,128},{128,0},{1,129},{129,1},{2,130},{130,2},{3,131},{131,3},{4... | collective-permute-start | bytes 6152 | tf_op jit(solution)/shard_map/ppermute | solution.py:21
  2.5 42.5 %collective-permute-start.2 = (s32[1,4,2,1,4]{4,3,2,1,0:T(1,128)S(1)}, s32[1,4,2,1,4]{4,3,2,1,0:T(1,128)S(1)}, u32[]{:S(2)}, u32[]{:S(2)}) collective-permute-start(s32[1,4,2,1,4]{4,3,2,1,0:T(1,128)S(1)} %compare_select_fusion.list_own), channel_id=1, source_target_pairs={{0,128},{128,0},{1,129},{129,1},{2,130},{130,2},{3,131},{131,3},{4... | collective-permute-start | bytes 392 | tf_op jit(solution)/shard_map/ppermute | solution.py:21
  2.6 0.8 copy-start.3
  3.4 43.0 %copy-start = (f32[1,3584]{1,0:T(1,128)S(1)}, f32[1,3584]{1,0:T(1,128)}, u32[]{:S(2)}) copy-start(f32[1,3584]{1,0:T(1,128)} %gain_own.3) | copy-start | bytes 43012
  3.4 43.0 %copy-start.1 = (f32[1,512]{1,0:T(1,128)S(1)}, f32[1,512]{1,0:T(1,128)}, u32[]{:S(2)}) copy-start(f32[1,512]{1,0:T(1,128)} %bias_own.3) | copy-start | bytes 6148
  45.1 1.3 copy-start.2
  54.2 23.7 %all-to-all-start.4 = ((bf16[16,16,3584]{2,1,0:T(8,128)(2,1)}), bf16[16,16,3584]{2,1,0:T(8,128)(2,1)S(1)}, u32[]{:S(2)}, u32[]{:S(2)}) async-start(bf16[16,16,3584]{2,1,0:T(8,128)(2,1)} %get-tuple-element.22), calls=%async_computation.4 | async-start | bytes 3670016 | tf_op jit(solution)/shard_map/all_to_all | solution.py:25

commit v4 on v3

--- a/solution.py
+++ b/solution.py
@@ -10,6 +10,7 @@
 BLK_DEV = 8
 BLOCK = 64
 PIECES = 4
+LANES = 128
 
 norm_eps = 1e-06
 
@@ -74,11 +75,31 @@
     return jnp.broadcast_to(row, (count, width))
 
 
+def folded(values):
+    quarter = values.shape[0] // 4
+    right = values[:, LANES:]
+    spare = LANES - right.shape[1]
+    last = right[3 * quarter :]
+    blocks = [
+        jnp.concatenate(
+            [right[index * quarter : (index + 1) * quarter], last[:, index * spare : (index + 1) * spare]], axis=1
+        )
+        for index in range(3)
+    ]
+    return jnp.concatenate([values[:, :LANES]] + blocks, axis=0)
+
+
+def right_part(blocks, width):
+    quarter = blocks.shape[0] // 3
+    last = [blocks[index * quarter : (index + 1) * quarter, width:] for index in range(3)]
+    return jnp.concatenate([blocks[:, :width], jnp.concatenate(last, axis=1)], axis=0)
+
+
 def first_layer(latents, dps, x_ref, gain_own, gain_other, bias_own, bias_other, list_own, list_other,
                 enc_own, enc_other, dec_own, dec_other,
-                part_hbm, active_ref, held_ref, enc, dec, share, enc_sems, dec_sems, share_sems):
-    group = x_ref.shape[1]
-    rows = dps * group
+                part_hbm, active_ref, held_ref, x, enc, dec, share, enc_sems, dec_sems, share_sems):
+    rows = x.shape[1]
+    group = rows // dps
     pair = group // latents
     cols = gain_own.shape[1]
     own_cols = cols // latents
@@ -90,16 +111,33 @@
     enc_copies = start_from(is_first, enc_own, enc_other, enc, enc_sems, 0)
     gain = jnp.where(is_first, gain_own[...], gain_other[...])
     bias = jnp.where(is_first, bias_own[...], bias_other[...])
-    step_latent = jnp.where(is_first, dps, 1)
-    step_dp = jnp.where(is_first, 1, latents)
-
-    def block(piece):
-        parts = [x_ref[piece * step_latent + dp * step_dp] for dp in range(dps)]
-        return jnp.concatenate(parts, axis=0)[:, :own_cols]
+    extra = own_cols - LANES
+    shard = x_ref.shape[0] // latents
+
+    @pl.when(is_first)
+    def _():
+        for piece in range(latents):
+            start = piece * shard
+            x[piece, :, pl.ds(0, LANES)] = x_ref[pl.ds(start, rows), :]
+            right = right_part(x_ref[pl.ds(start + rows, shard - rows), :].astype(f32), extra)
+            x[piece, :, pl.ds(LANES, extra)] = right.astype(bf16)
+
+    @pl.when(jnp.logical_not(is_first))
+    def _():
+        shard = x_ref.shape[0] // dps
+        whole = latents * group
+        for dp in range(dps):
+            start = dp * shard
+            right = right_part(x_ref[pl.ds(start + whole, shard - whole), :].astype(f32), extra).astype(bf16)
+            for piece in range(latents):
+                mine = slice(piece * group, (piece + 1) * group)
+                to = pl.ds(dp * group, group)
+                x[piece, to, pl.ds(0, LANES)] = x_ref[pl.ds(start + piece * group, group), :]
+                x[piece, to, pl.ds(LANES, extra)] = right[mine]
 
     squares = jnp.zeros((rows, own_cols), f32)
     for piece in range(latents):
-        values = block(piece).astype(f32)
+        values = x[piece].astype(f32)
         squares += values * values
     scaling = lax.rsqrt(jnp.sum(squares, axis=1, keepdims=True) / cols + norm_eps)
 
@@ -114,7 +152,7 @@
             if piece == 0:
                 dec_copies = start_from(is_first, dec_own, dec_other, dec, dec_sems, 1)
         own_gain = gain[:, piece * own_cols : (piece + 1) * own_cols]
-        values = block(piece)
+        values = x[piece]
         held_ref[piece] = dot(choose_own, values).astype(bf16)
         normed = (values.astype(f32) * scaling * own_gain).astype(bf16)
         total += dot(normed, enc[pl.ds(piece * own_cols, own_cols), :])
@@ -168,23 +206,27 @@
         copy.wait()
 
 
-def cross_share(active_ref, cross_hbm, cross_out, cross, cross_part, cross_sems, out_sem):
+def cross_share(own_segment, *refs):
+    active_ref, *_, cross_hbm, cross_out, cross, cross_part, cross_sems, out_sem = refs
     latents, _, own_cols = cross_out.shape
-    cross_copies = copies(cross_hbm, cross, cross_sems, 1)
-    for copy in cross_copies:
-        copy.start()
     size = cross.shape[1] // PIECES
     per_piece = latents // PIECES
-    earlier = active_ref[...]
-    for piece in range(PIECES):
-        cross_copies[piece].wait()
-        share = dot(earlier, cross[:, pl.ds(piece * size, size)])
-        for inner in range(per_piece):
-            where = slice(inner * own_cols, (inner + 1) * own_cols)
-            cross_part[piece * per_piece + inner] = share[:, where]
-    copy = pltpu.make_async_copy(cross_part, cross_out, out_sem)
-    copy.start()
-    copy.wait()
+
+    @pl.when(lax.axis_index("segment") == own_segment)
+    def _():
+        cross_copies = copies(cross_hbm, cross, cross_sems, 1)
+        for copy in cross_copies:
+            copy.start()
+        earlier = active_ref[...]
+        for piece in range(PIECES):
+            cross_copies[piece].wait()
+            share = dot(earlier, cross[:, pl.ds(piece * size, size)])
+            for inner in range(per_piece):
+                where = slice(inner * own_cols, (inner + 1) * own_cols)
+                cross_part[piece * per_piece + inner] = share[:, where]
+        copy = pltpu.make_async_copy(cross_part, cross_out, out_sem)
+        copy.start()
+        copy.wait()
 
 
 def second_layer(dps, x_ref, recon_ref, bias_own, bias_other, list_own, list_other,
@@ -226,8 +268,14 @@
         if piece % (latents // PIECES) == 0:
             dec_copies[piece // (latents // PIECES)].wait()
             cross_copies[piece // (latents // PIECES)].wait()
-        out_ref[piece, pl.ds(0, rows), :] = (dot(sorted_active, dec[piece]) + cross[piece]).astype(bf16)
-        out_ref[piece, pl.ds(rows, some), :] = recon_ref[piece]
+        share = folded(dot(sorted_active, dec[piece]) + cross[piece]).astype(bf16)
+        recon = recon_ref[piece]
+        extra = recon.shape[1] - LANES
+        filled = share.shape[0]
+        out_ref[piece, pl.ds(0, filled), :] = share
+        out_ref[piece, pl.ds(filled, some), :] = recon[:, :LANES]
+        out_ref[piece, pl.ds(filled + some, some), pl.ds(0, extra)] = recon[:, LANES:]
+        out_ref[piece, pl.ds(filled + some, some), pl.ds(extra, LANES - extra)] = jnp.zeros((some, LANES - extra), bf16)
 
 
 def take_own(x_ref, out_ref):
@@ -242,9 +290,10 @@
             out_ref[piece, pl.ds(batch * mine.shape[0], mine.shape[0]), :] = mine
 
 
-def repeat(x_ref, out_ref):
+def repeat(own_cols, x_ref, out_ref):
+    values = folded(x_ref[...].astype(f32)[:, :own_cols]).astype(bf16)
     for piece in range(out_ref.shape[0]):
-        out_ref[piece] = x_ref[...]
+        out_ref[piece] = values
 
 
 def sum_parts(x_ref, out_ref):
@@ -287,19 +336,24 @@
 
 
 def sum_for_dp(rows, dps, pair, x_ref, out_ref):
-    latents, taken, own_cols = x_ref.shape
-    total = x_ref[0, pl.ds(0, rows), :].astype(f32)
+    latents = x_ref.shape[0]
+    some = dps * pair
+    filled = x_ref.shape[1] - 2 * some
+    own_cols = out_ref.shape[3]
+    extra = own_cols - LANES
+    total = x_ref[0, pl.ds(0, filled), :].astype(f32)
     for source in range(1, latents):
-        total += x_ref[source, pl.ds(0, rows), :].astype(f32)
+        total += x_ref[source, pl.ds(0, filled), :].astype(f32)
+    total = jnp.concatenate([total[:rows], right_part(total[rows:], extra)], axis=1)
     out_ref[1] = total.astype(bf16).reshape(dps, rows // dps, own_cols)
-    extra = taken - rows
     dp = lax.axis_index("dp")
     choose_own = one_hot(
-        (latents * pair, latents * extra),
-        lambda row: (row // pair) * extra + dp * pair + row % pair,
-    )
-    recon = x_ref[:, pl.ds(rows, extra), :].reshape(latents * extra, own_cols)
-    recon = dot(choose_own, recon).astype(bf16)
+        (latents * pair, latents * some),
+        lambda row: (row // pair) * some + dp * pair + row % pair,
+    )
+    left = x_ref[:, pl.ds(filled, some), :].reshape(latents * some, LANES)
+    right = x_ref[:, pl.ds(filled + some, some), :].reshape(latents * some, LANES)
+    recon = jnp.concatenate([dot(choose_own, left), dot(choose_own, right)[:, :extra]], axis=1).astype(bf16)
     for piece in range(dps):
         out_ref[0, piece] = recon
 
@@ -364,14 +418,16 @@
     def dp_first(resid):
         mine = call(take_own, array((dps, group, padded)), [resid])
         some_rows = exchanged(mine, "dp").reshape(rows, padded)
-        every = call(repeat, array((latents, rows, padded)), [some_rows])
-        return exchanged(every, "latent").reshape(latents * dps, group, padded)
+        every = call(functools.partial(repeat, own_cols), array((latents, rows * 7 // 4, LANES)), [some_rows])
+        return exchanged(every, "latent").reshape(-1, LANES)
 
     def latent_first(resid):
         mine = call(take_own, array((latents, group, padded)), [resid])
         some_cols = exchanged(mine, "latent").reshape(latents * group, padded)
-        every = call(repeat, array((dps, latents * group, padded)), [some_cols])
-        return exchanged(every, "dp").reshape(latents * dps, group, padded)
+        every = call(
+            functools.partial(repeat, own_cols), array((dps, latents * group * 7 // 4, LANES)), [some_cols]
+        )
+        return exchanged(every, "dp").reshape(-1, LANES)
 
     resid0 = lax.cond(is_first, dp_first, latent_first, resid_in)
 
@@ -383,7 +439,7 @@
         [resid0] + gains + biases + lists + weights,
         scalars=2,
         hbm=4,
-        scratch=[enc_space, dec_space, pltpu.VMEM((latents, some, cols), bf16)] + [sems] * 3,
+        scratch=[pltpu.VMEM((latents, rows, own_cols), bf16), enc_space, dec_space, pltpu.VMEM((latents, some, cols), bf16)] + [sems] * 3,
         limit=26,
         hbm_outs=1,
     )
@@ -394,18 +450,15 @@
     dec_cut = array((latents, width, own_cols), space=pltpu.HBM)
     cut_space = dict(scratch=[dec_space, dec_parts, sems, one_sem], limit=24, hbm_outs=1)
     dec1 = call(functools.partial(cut_decoder, 1), [dec_cut], [dec_own], hbm=1, **cut_space)[0]
-    partial0, dec1 = lax.optimization_barrier((partial0, dec1))
+    cross_cut = array((latents, rows, own_cols), f32, space=pltpu.HBM)
+    cross_space = dict(scratch=[dec_space, cross_parts, sems, one_sem], limit=24, hbm_outs=1)
+    cross0 = call(functools.partial(cross_share, 1), [cross_cut], [active0, dec_cross], hbm=1, **cross_space)[0]
+    partial0, dec1, cross0 = lax.optimization_barrier((partial0, dec1, cross0))
     dec1 = call(
         functools.partial(cut_decoder, 0), [dec_cut], [dec1, weights[3]], hbm=2, aliases={0: 0}, **cut_space
     )[0]
     cross0 = call(
-        cross_share,
-        [array((latents, rows, own_cols), f32, space=pltpu.HBM)],
-        [active0, dec_cross],
-        hbm=1,
-        scratch=[dec_space, cross_parts, sems, one_sem],
-        limit=24,
-        hbm_outs=1,
+        functools.partial(cross_share, 0), [cross_cut], [active0, cross0, dec_cross], hbm=2, aliases={1: 0}, **cross_space
     )[0]
     down = 2
     block = (dps, some // down, cols * down // dps)
@@ -423,7 +476,7 @@
 
     outgoing = call(
         functools.partial(second_layer, dps),
-        array((latents, rows + some, own_cols)),
+        array((latents, rows * 7 // 4 + 2 * some, LANES)),
         [normed1, recon0] + biases + lists + weights[:2] + [dec1, cross0],
         scalars=2,
         hbm=4,

time: 185 us -> 172 us (0.930)
  blocking collectives: 140 us -> 131 us
    all_to_all x7, blocking collectives: 140 us -> 131 us  [exchanged(): return lax.all_to_all(value, axis, 0, 0)]
    pallas_call x12 -> x13, Pallas kernels: 26.1 us -> 24.9 us  [call(): pl.pallas_call(kernel, out_shape=outs, in_specs=specs, out_specs=vmem if...]
where the time goes in v4:
time: 172 us
  blocking collectives  131 us (76%)
  Pallas kernels  24.9 us (14%)
  waiting for transfers between devices  8.45 us (5%)
  starting transfers between devices  4.82 us (3%)
    all_to_all x7, blocking collectives, exchanged(): return lax.all_to_all(value, axis, 0, 0)  131 us
    pallas_call x13, Pallas kernels, call(): pl.pallas_call(kernel, out_shape=outs, in_specs=specs, out_specs=vmem if...  24.9 us
    all_to_all x1, waiting for transfers between devices, exchanged(): return lax.all_to_all(value, axis, 0, 0)  8.44 us
    all_to_all x1, starting transfers between devices, exchanged(): return lax.all_to_all(value, axis, 0, 0)  3.72 us
  transfers between devices with their start and end apart: 6, of which 1 were waited for; matrix products, arithmetic and copies ran while one was open for 1% of the time, Pallas kernels for 6%

profile of v4, /device:TPU:32, one launch (start us, length us, event | category | flops | bytes accessed | tf_op | source)
XLA Modules:
  0.0 171.8 jit_solution(6057831279380707128)
XLA Ops:
  0.0 0.5 collective-permute-start.4
  0.5 0.5 collective-permute-start
  1.0 0.8 copy.11
  1.8 0.8 compare_select_fusion.list_own
  2.7 0.7 copy-done.2
  3.4 40.3 %conditional.1 = (bf16[7168,128]{1,0:T(8,128)(2,1)S(1)}) conditional(s32[]{:T(128)} %convert_element_type.3, bf16[4,16,224]{2,1,0:T(8,128)(2,1)S(1)} %copy-done.2, bf16[4,16,224]{2,1,0:T(8,128)(2,1)S(1)} %copy-done.2), branch_computations={%region_0.1_spmd, %region_1.2_spmd} | conditional | bytes 4194312 | solution.py:432
  3.4 16.0 %all_to_all.48 = bf16[8,32,256]{2,1,0:T(8,128)(2,1)S(1)} all-to-all(bf16[8,32,256]{2,1,0:T(8,128)(2,1)S(1)} %branch_1_fun.2), channel_id=1, replica_groups=mesh['segment'=2,'latent'=16,'dp'=8] {'dp'}, dimensions={0} | all-to-all | bytes 262144 | tf_op jit(solution)/shard_map/cond/branch_1_fun/all_to_all | solution.py:26
  19.4 0.2 branch_1_fun.3
  19.6 24.1 %all_to_all.49 = bf16[16,448,128]{2,1,0:T(8,128)(2,1)S(1)} all-to-all(bf16[16,448,128]{2,1,0:T(8,128)(2,1)S(1)} %branch_1_fun.3), channel_id=1, replica_groups=mesh['segment'=2,'latent'=16,'dp'=8] {'latent'}, dimensions={0} | all-to-all | bytes 3670016 | tf_op jit(solution)/shard_map/cond/branch_1_fun/all_to_all | solution.py:26
  43.8 6.5 %shard_map.88 = (bf16[16,16,3584]{2,1,0:T(8,128)(2,1)}, bf16[256,512]{1,0:T(8,128)(2,1)S(1)}, bf16[16,16,224]{2,1,0:T(8,128)(2,1)S(1)}) custom-call(bf16[7168,128]{1,0:T(8,128)(2,1)S(1)} %get-tuple-element.34.x_ref, f32[1,3584]{1,0:T(1,128)S(1)} %copy-done, f32[1,3584]{1,0:T(1,128)S(1)} %collective-permute-done.gain_other, f32[1,512]{1,0:T(1,128)S(1)} %copy-done.1, ...), custom_call_target="tpu_custom_call" | custom-call | tf_op jit(solution)/shard_map/pallas_call | solution.py:379
  50.3 3.7 %all-to-all-start.4 = ((bf16[16,16,3584]{2,1,0:T(8,128)(2,1)}), bf16[16,16,3584]{2,1,0:T(8,128)(2,1)S(1)}, u32[]{:S(2)}, u32[]{:S(2)}) async-start(bf16[16,16,3584]{2,1,0:T(8,128)(2,1)} %get-tuple-element.24), calls=%async_computation.4 | async-start | bytes 3670016 | tf_op jit(solution)/shard_map/all_to_all | solution.py:26
  54.3 5.7 %shard_map.92.cross_hbm = f32[16,256,224]{2,1,0:T(8,128)} custom-call(bf16[256,512]{1,0:T(8,128)(2,1)S(1)} %get-tuple-element.23.refs_0_, f32[16,256,224]{2,1,0:T(8,128)} %shard_map.90.refs_1_, bf16[512,3584]{1,0:T(8,128)(2,1)} %refs_2_.1), custom_call_target="tpu_custom_call", output_to_operand_aliasing={{}: (1, {})} | custom-call | tf_op jit(solution)/shard_map/pallas_call | solution.py:379
  60.0 4.8 %shard_map.91.dec_hbm = bf16[16,512,224]{2,1,0:T(8,128)(2,1)} custom-call(bf16[16,512,224]{2,1,0:T(8,128)(2,1)} %shard_map.89.refs_0_, bf16[512,3584]{1,0:T(8,128)(2,1)} %collective-permute-done.4.dec_other.refs_1_), custom_call_target="tpu_custom_call", output_to_operand_aliasing={{}: (0, {})} | custom-call | tf_op jit(solution)/shard_map/pallas_call | solution.py:379
  64.8 8.4 %all-to-all-done.4.x_ref = bf16[16,16,3584]{2,1,0:T(8,128)(2,1)S(1)} async-done(((bf16[16,16,3584]{2,1,0:T(8,128)(2,1)}), bf16[16,16,3584]{2,1,0:T(8,128)(2,1)S(1)}, u32[]{:S(2)}, u32[]{:S(2)}) %all-to-all-start.4) | async-done | bytes 1835040 | tf_op jit(solution)/shard_map/all_to_all | solution.py:26
  73.2 0.2 shard_map.93
  73.5 12.3 %all_to_all.50.x_ref = f32[8,8,896]{2,1,0:T(8,128)S(1)} all-to-all(f32[8,8,896]{2,1,0:T(8,128)S(1)} %shard_map.93), channel_id=1, replica_groups=mesh['segment'=2,'latent'=16,'dp'=8] {'dp'}, dimensions={0} | all-to-all | bytes 458752 | tf_op jit(solution)/shard_map/all_to_all | solution.py:26
  85.8 12.5 %all_to_all.51.pieces_ref = f32[8,8,896]{2,1,0:T(8,128)S(1)} all-to-all(f32[8,8,896]{2,1,0:T(8,128)S(1)} %shard_map.94), channel_id=1, replica_groups=mesh['segment'=2,'latent'=16,'dp'=8] {'dp'}, dimensions={0} | all-to-all | bytes 458752 | tf_op jit(solution)/shard_map/all_to_all | solution.py:26
  98.3 0.3 shard_map.95
  98.6 20.4 %all_to_all.52.x_ref = bf16[16,16,3584]{2,1,0:T(8,128)(2,1)S(1)} all-to-all(bf16[16,16,3584]{2,1,0:T(8,128)(2,1)S(1)} %get-tuple-element.30), channel_id=1, replica_groups=mesh['segment'=2,'latent'=16,'dp'=8] {'latent'}, dimensions={0} | all-to-all | bytes 3670016 | tf_op jit(solution)/shard_map/all_to_all | solution.py:26
  119.0 6.1 %shard_map.96 = bf16[16,480,128]{2,1,0:T(8,128)(2,1)S(1)} custom-call(bf16[16,16,3584]{2,1,0:T(8,128)(2,1)S(1)} %all_to_all.52.x_ref, bf16[16,16,224]{2,1,0:T(8,128)(2,1)S(1)} %get-tuple-element.31.recon_ref, f32[1,512]{1,0:T(1,128)S(1)} %copy-done.1, f32[1,512]{1,0:T(1,128)S(1)} %collective-permute-done.1.bias_other, ...), custom_call_target="tpu_custom_call" | custom-call | tf_op jit(solution)/shard_map/pallas_call | solution.py:379
  125.1 21.1 %all_to_all.53.x_ref = bf16[16,480,128]{2,1,0:T(8,128)(2,1)S(1)} all-to-all(bf16[16,480,128]{2,1,0:T(8,128)(2,1)S(1)} %shard_map.96), channel_id=1, replica_groups=mesh['segment'=2,'latent'=16,'dp'=8] {'latent'}, dimensions={0} | all-to-all | bytes 3932160 | tf_op jit(solution)/shard_map/all_to_all | solution.py:26
  146.2 0.3 shard_map.97
  146.5 24.7 %all_to_all.54 = bf16[16,32,224]{2,1,0:T(8,128)(2,1)S(1)} all-to-all(bf16[16,32,224]{2,1,0:T(8,128)(2,1)S(1)} %bitcast.11), channel_id=1, replica_groups=mesh['segment'=2,'latent'=16,'dp'=8] {'segment','dp'}, dimensions={0} | all-to-all | bytes 458752 | tf_op jit(solution)/shard_map/all_to_all | solution.py:26
  171.2 0.7 shard_map.98
  (19 shorter events, 0.5 us)
Async XLA Ops:
  0.0 43.7 %collective-permute-start.3 = (bf16[3584,512]{1,0:T(8,128)(2,1)}, bf16[3584,512]{1,0:T(8,128)(2,1)}, u32[]{:S(2)}, u32[]{:S(2)}) collective-permute-start(bf16[3584,512]{1,0:T(8,128)(2,1)} %bitcast.16), channel_id=1, source_target_pairs={{0,128},{128,0},{1,129},{129,1},{2,130},{130,2},{3,131},{131,3},{4... | collective-permute-start | bytes 11010056 | tf_op jit(solution)/shard_map/ppermute | solution.py:22
  0.0 43.7 %collective-permute-start.4 = (bf16[512,3584]{1,0:T(8,128)(2,1)}, bf16[512,3584]{1,0:T(8,128)(2,1)}, u32[]{:S(2)}, u32[]{:S(2)}) collective-permute-start(bf16[512,3584]{1,0:T(8,128)(2,1)} %bitcast.19), channel_id=1, source_target_pairs={{0,128},{128,0},{1,129},{129,1},{2,130},{130,2},{3,131},{131,3},{4... | collective-permute-start | bytes 11010056 | tf_op jit(solution)/shard_map/ppermute | solution.py:22
  0.5 43.2 %collective-permute-start.1 = (f32[1,512]{1,0:T(1,128)}, f32[1,512]{1,0:T(1,128)S(1)}, u32[]{:S(2)}, u32[]{:S(2)}) collective-permute-start(f32[1,512]{1,0:T(1,128)} %bias_own.3), channel_id=1, source_target_pairs={{0,128},{128,0},{1,129},{129,1},{2,130},{130,2},{3,131},{131,3},{4... | collective-permute-start | bytes 6152 | tf_op jit(solution)/shard_map/ppermute | solution.py:22
  0.5 43.2 %collective-permute-start = (f32[1,3584]{1,0:T(1,128)}, f32[1,3584]{1,0:T(1,128)S(1)}, u32[]{:S(2)}, u32[]{:S(2)}) collective-permute-start(f32[1,3584]{1,0:T(1,128)} %gain_own.3), channel_id=1, source_target_pairs={{0,128},{128,0},{1,129},{129,1},{2,130},{130,2},{3,131},{131,3},{4... | collective-permute-start | bytes 43016 | tf_op jit(solution)/shard_map/ppermute | solution.py:22
  2.5 41.2 %collective-permute-start.2 = (s32[1,4,2,1,4]{4,3,2,1,0:T(1,128)S(1)}, s32[1,4,2,1,4]{4,3,2,1,0:T(1,128)S(1)}, u32[]{:S(2)}, u32[]{:S(2)}) collective-permute-start(s32[1,4,2,1,4]{4,3,2,1,0:T(1,128)S(1)} %compare_select_fusion.list_own), channel_id=1, source_target_pairs={{0,128},{128,0},{1,129},{129,1},{2,130},{130,2},{3,131},{131,3},{4... | collective-permute-start | bytes 392 | tf_op jit(solution)/shard_map/ppermute | solution.py:22
  2.6 0.8 copy-start.2
  3.4 40.4 %copy-start = (f32[1,3584]{1,0:T(1,128)S(1)}, f32[1,3584]{1,0:T(1,128)}, u32[]{:S(2)}) copy-start(f32[1,3584]{1,0:T(1,128)} %gain_own.3) | copy-start | bytes 43012
  3.4 40.4 %copy-start.1 = (f32[1,512]{1,0:T(1,128)S(1)}, f32[1,512]{1,0:T(1,128)}, u32[]{:S(2)}) copy-start(f32[1,512]{1,0:T(1,128)} %bias_own.3) | copy-start | bytes 6148
  50.3 22.9 %all-to-all-start.4 = ((bf16[16,16,3584]{2,1,0:T(8,128)(2,1)}), bf16[16,16,3584]{2,1,0:T(8,128)(2,1)S(1)}, u32[]{:S(2)}, u32[]{:S(2)}) async-start(bf16[16,16,3584]{2,1,0:T(8,128)(2,1)} %get-tuple-element.24), calls=%async_computation.4 | async-start | bytes 3670016 | tf_op jit(solution)/shard_map/all_to_all | solution.py:26

commit v5 on v4

--- a/solution.py
+++ b/solution.py
@@ -185,7 +185,7 @@
 
 
 def cut_decoder(own_segment, *refs):
-    *_, dec_hbm, dec_out, dec, dec_part, dec_sems, out_sem = refs
+    *_, dec_hbm, dec_out, dec, dec_part, dec_sems, out_sems = refs
     latents, _, own_cols = dec_out.shape
     size = dec.shape[1] // PIECES
     per_piece = latents // PIECES
@@ -193,6 +193,7 @@
     @pl.when(lax.axis_index("segment") == own_segment)
     def _():
         dec_copies = copies(dec_hbm, dec, dec_sems, 1)
+        sent = copies(dec_part, dec_out, out_sems, 0)
         for copy in dec_copies:
             copy.start()
         for piece in range(PIECES):
@@ -201,13 +202,13 @@
             for inner in range(per_piece):
                 where = slice(inner * own_cols, (inner + 1) * own_cols)
                 dec_part[piece * per_piece + inner] = decoder[:, where].astype(bf16)
-        copy = pltpu.make_async_copy(dec_part, dec_out, out_sem)
-        copy.start()
-        copy.wait()
+            sent[piece].start()
+        for copy in sent:
+            copy.wait()
 
 
 def cross_share(own_segment, *refs):
-    active_ref, *_, cross_hbm, cross_out, cross, cross_part, cross_sems, out_sem = refs
+    active_ref, *_, cross_hbm, cross_out, cross, cross_part, cross_sems, out_sems = refs
     latents, _, own_cols = cross_out.shape
     size = cross.shape[1] // PIECES
     per_piece = latents // PIECES
@@ -215,6 +216,7 @@
     @pl.when(lax.axis_index("segment") == own_segment)
     def _():
         cross_copies = copies(cross_hbm, cross, cross_sems, 1)
+        sent = copies(cross_part, cross_out, out_sems, 0)
         for copy in cross_copies:
             copy.start()
         earlier = active_ref[...]
@@ -224,9 +226,9 @@
             for inner in range(per_piece):
                 where = slice(inner * own_cols, (inner + 1) * own_cols)
                 cross_part[piece * per_piece + inner] = share[:, where]
-        copy = pltpu.make_async_copy(cross_part, cross_out, out_sem)
-        copy.start()
-        copy.wait()
+            sent[piece].start()
+        for copy in sent:
+            copy.wait()
 
 
 def second_layer(dps, x_ref, recon_ref, bias_own, bias_other, list_own, list_other,
@@ -446,12 +448,12 @@
     held = held.transpose(1, 0, 2).reshape(some, cols)
     dec_parts = pltpu.VMEM((latents, width, own_cols), bf16)
     cross_parts = pltpu.VMEM((latents, rows, own_cols), f32)
-    one_sem = pltpu.SemaphoreType.DMA(())
+    out_sems = pltpu.SemaphoreType.DMA((PIECES,))
     dec_cut = array((latents, width, own_cols), space=pltpu.HBM)
-    cut_space = dict(scratch=[dec_space, dec_parts, sems, one_sem], limit=24, hbm_outs=1)
+    cut_space = dict(scratch=[dec_space, dec_parts, sems, out_sems], limit=24, hbm_outs=1)
     dec1 = call(functools.partial(cut_decoder, 1), [dec_cut], [dec_own], hbm=1, **cut_space)[0]
     cross_cut = array((latents, rows, own_cols), f32, space=pltpu.HBM)
-    cross_space = dict(scratch=[dec_space, cross_parts, sems, one_sem], limit=24, hbm_outs=1)
+    cross_space = dict(scratch=[dec_space, cross_parts, sems, out_sems], limit=24, hbm_outs=1)
     cross0 = call(functools.partial(cross_share, 1), [cross_cut], [active0, dec_cross], hbm=1, **cross_space)[0]
     partial0, dec1, cross0 = lax.optimization_barrier((partial0, dec1, cross0))
     dec1 = call(

time: 172 us -> 174 us (1.012)
  blocking collectives: 131 us -> 133 us
  waiting for transfers between devices: 8.45 us -> 10.3 us
  Pallas kernels: 24.9 us -> 23.1 us
    all_to_all x1, waiting for transfers between devices: 8.44 us -> 10.3 us  [exchanged(): return lax.all_to_all(value, axis, 0, 0)]
    all_to_all x7, blocking collectives: 131 us -> 133 us  [exchanged(): return lax.all_to_all(value, axis, 0, 0)]
    pallas_call x13, Pallas kernels: 24.9 us -> 23.1 us  [call(): pl.pallas_call(kernel, out_shape=outs, in_specs=specs, out_specs=vmem if...]
  transfers between devices with their start and end apart: 6 -> 6, of which waited for: 1 -> 1; matrix products, arithmetic and copies ran while one was open for 1% -> 1% of each run, Pallas kernels for 6% -> 5%
where the time goes in v5:
time: 174 us
  blocking collectives  133 us (76%)
  Pallas kernels  23.1 us (13%)
  waiting for transfers between devices  10.3 us (6%)
  starting transfers between devices  4.82 us (3%)
    all_to_all x7, blocking collectives, exchanged(): return lax.all_to_all(value, axis, 0, 0)  133 us
    pallas_call x13, Pallas kernels, call(): pl.pallas_call(kernel, out_shape=outs, in_specs=specs, out_specs=vmem if...  23.1 us
    all_to_all x1, waiting for transfers between devices, exchanged(): return lax.all_to_all(value, axis, 0, 0)  10.3 us
    all_to_all x1, starting transfers between devices, exchanged(): return lax.all_to_all(value, axis, 0, 0)  3.72 us
  transfers between devices with their start and end apart: 6, of which 1 were waited for; matrix products, arithmetic and copies ran while one was open for 1% of the time, Pallas kernels for 5%

profile of v5, /device:TPU:32, one launch (start us, length us, event | category | flops | bytes accessed | tf_op | source)
XLA Modules:
  0.0 173.7 jit_solution(12499406456758688271)
XLA Ops:
  0.0 0.5 collective-permute-start.4
  0.5 0.5 collective-permute-start
  1.0 0.8 copy.11
  1.8 0.8 compare_select_fusion.list_own
  2.7 0.6 copy-done.2
  3.4 40.3 %conditional.1 = (bf16[7168,128]{1,0:T(8,128)(2,1)S(1)}) conditional(s32[]{:T(128)} %convert_element_type.3, bf16[4,16,224]{2,1,0:T(8,128)(2,1)S(1)} %copy-done.2, bf16[4,16,224]{2,1,0:T(8,128)(2,1)S(1)} %copy-done.2), branch_computations={%region_0.1_spmd, %region_1.2_spmd} | conditional | bytes 4194312 | solution.py:434
  3.4 16.0 %all_to_all.48 = bf16[8,32,256]{2,1,0:T(8,128)(2,1)S(1)} all-to-all(bf16[8,32,256]{2,1,0:T(8,128)(2,1)S(1)} %branch_1_fun.2), channel_id=1, replica_groups=mesh['segment'=2,'latent'=16,'dp'=8] {'dp'}, dimensions={0} | all-to-all | bytes 262144 | tf_op jit(solution)/shard_map/cond/branch_1_fun/all_to_all | solution.py:26
  19.4 0.2 branch_1_fun.3
  19.6 24.1 %all_to_all.49 = bf16[16,448,128]{2,1,0:T(8,128)(2,1)S(1)} all-to-all(bf16[16,448,128]{2,1,0:T(8,128)(2,1)S(1)} %branch_1_fun.3), channel_id=1, replica_groups=mesh['segment'=2,'latent'=16,'dp'=8] {'latent'}, dimensions={0} | all-to-all | bytes 3670016 | tf_op jit(solution)/shard_map/cond/branch_1_fun/all_to_all | solution.py:26
  43.8 6.5 %shard_map.88 = (bf16[16,16,3584]{2,1,0:T(8,128)(2,1)}, bf16[256,512]{1,0:T(8,128)(2,1)S(1)}, bf16[16,16,224]{2,1,0:T(8,128)(2,1)S(1)}) custom-call(bf16[7168,128]{1,0:T(8,128)(2,1)S(1)} %get-tuple-element.34.x_ref, f32[1,3584]{1,0:T(1,128)S(1)} %copy-done, f32[1,3584]{1,0:T(1,128)S(1)} %collective-permute-done.gain_other, f32[1,512]{1,0:T(1,128)S(1)} %copy-done.1, ...), custom_call_target="tpu_custom_call" | custom-call | tf_op jit(solution)/shard_map/pallas_call | solution.py:381
  50.4 3.7 %all-to-all-start.4 = ((bf16[16,16,3584]{2,1,0:T(8,128)(2,1)}), bf16[16,16,3584]{2,1,0:T(8,128)(2,1)S(1)}, u32[]{:S(2)}, u32[]{:S(2)}) async-start(bf16[16,16,3584]{2,1,0:T(8,128)(2,1)} %get-tuple-element.24), calls=%async_computation.4 | async-start | bytes 3670016 | tf_op jit(solution)/shard_map/all_to_all | solution.py:26
  54.3 4.8 %shard_map.92.cross_hbm = f32[16,256,224]{2,1,0:T(8,128)} custom-call(bf16[256,512]{1,0:T(8,128)(2,1)S(1)} %get-tuple-element.23.refs_0_, f32[16,256,224]{2,1,0:T(8,128)} %shard_map.90.refs_1_, bf16[512,3584]{1,0:T(8,128)(2,1)} %refs_2_.1), custom_call_target="tpu_custom_call", output_to_operand_aliasing={{}: (1, {})} | custom-call | tf_op jit(solution)/shard_map/pallas_call | solution.py:381
  59.1 3.9 %shard_map.91.dec_hbm = bf16[16,512,224]{2,1,0:T(8,128)(2,1)} custom-call(bf16[16,512,224]{2,1,0:T(8,128)(2,1)} %shard_map.89.refs_0_, bf16[512,3584]{1,0:T(8,128)(2,1)} %collective-permute-done.4.dec_other.refs_1_), custom_call_target="tpu_custom_call", output_to_operand_aliasing={{}: (0, {})} | custom-call | tf_op jit(solution)/shard_map/pallas_call | solution.py:381
  63.0 10.3 %all-to-all-done.4.x_ref = bf16[16,16,3584]{2,1,0:T(8,128)(2,1)S(1)} async-done(((bf16[16,16,3584]{2,1,0:T(8,128)(2,1)}), bf16[16,16,3584]{2,1,0:T(8,128)(2,1)S(1)}, u32[]{:S(2)}, u32[]{:S(2)}) %all-to-all-start.4) | async-done | bytes 1835040 | tf_op jit(solution)/shard_map/all_to_all | solution.py:26
  73.3 0.2 shard_map.93
  73.5 12.3 %all_to_all.50.x_ref = f32[8,8,896]{2,1,0:T(8,128)S(1)} all-to-all(f32[8,8,896]{2,1,0:T(8,128)S(1)} %shard_map.93), channel_id=1, replica_groups=mesh['segment'=2,'latent'=16,'dp'=8] {'dp'}, dimensions={0} | all-to-all | bytes 458752 | tf_op jit(solution)/shard_map/all_to_all | solution.py:26
  85.9 14.9 %all_to_all.51.pieces_ref = f32[8,8,896]{2,1,0:T(8,128)S(1)} all-to-all(f32[8,8,896]{2,1,0:T(8,128)S(1)} %shard_map.94), channel_id=1, replica_groups=mesh['segment'=2,'latent'=16,'dp'=8] {'dp'}, dimensions={0} | all-to-all | bytes 458752 | tf_op jit(solution)/shard_map/all_to_all | solution.py:26
  100.8 0.3 shard_map.95
  101.1 20.5 %all_to_all.52.x_ref = bf16[16,16,3584]{2,1,0:T(8,128)(2,1)S(1)} all-to-all(bf16[16,16,3584]{2,1,0:T(8,128)(2,1)S(1)} %get-tuple-element.30), channel_id=1, replica_groups=mesh['segment'=2,'latent'=16,'dp'=8] {'latent'}, dimensions={0} | all-to-all | bytes 3670016 | tf_op jit(solution)/shard_map/all_to_all | solution.py:26
  121.5 6.1 %shard_map.96 = bf16[16,480,128]{2,1,0:T(8,128)(2,1)S(1)} custom-call(bf16[16,16,3584]{2,1,0:T(8,128)(2,1)S(1)} %all_to_all.52.x_ref, bf16[16,16,224]{2,1,0:T(8,128)(2,1)S(1)} %get-tuple-element.31.recon_ref, f32[1,512]{1,0:T(1,128)S(1)} %copy-done.1, f32[1,512]{1,0:T(1,128)S(1)} %collective-permute-done.1.bias_other, ...), custom_call_target="tpu_custom_call" | custom-call | tf_op jit(solution)/shard_map/pallas_call | solution.py:381
  127.7 22.6 %all_to_all.53.x_ref = bf16[16,480,128]{2,1,0:T(8,128)(2,1)S(1)} all-to-all(bf16[16,480,128]{2,1,0:T(8,128)(2,1)S(1)} %shard_map.96), channel_id=1, replica_groups=mesh['segment'=2,'latent'=16,'dp'=8] {'latent'}, dimensions={0} | all-to-all | bytes 3932160 | tf_op jit(solution)/shard_map/all_to_all | solution.py:26
  150.2 0.3 shard_map.97
  150.5 22.5 %all_to_all.54 = bf16[16,32,224]{2,1,0:T(8,128)(2,1)S(1)} all-to-all(bf16[16,32,224]{2,1,0:T(8,128)(2,1)S(1)} %bitcast.11), channel_id=1, replica_groups=mesh['segment'=2,'latent'=16,'dp'=8] {'segment','dp'}, dimensions={0} | all-to-all | bytes 458752 | tf_op jit(solution)/shard_map/all_to_all | solution.py:26
  173.0 0.7 shard_map.98
  (19 shorter events, 0.5 us)
Async XLA Ops:
  0.0 43.7 %collective-permute-start.3 = (bf16[3584,512]{1,0:T(8,128)(2,1)}, bf16[3584,512]{1,0:T(8,128)(2,1)}, u32[]{:S(2)}, u32[]{:S(2)}) collective-permute-start(bf16[3584,512]{1,0:T(8,128)(2,1)} %bitcast.16), channel_id=1, source_target_pairs={{0,128},{128,0},{1,129},{129,1},{2,130},{130,2},{3,131},{131,3},{4... | collective-permute-start | bytes 11010056 | tf_op jit(solution)/shard_map/ppermute | solution.py:22
  0.0 43.7 %collective-permute-start.4 = (bf16[512,3584]{1,0:T(8,128)(2,1)}, bf16[512,3584]{1,0:T(8,128)(2,1)}, u32[]{:S(2)}, u32[]{:S(2)}) collective-permute-start(bf16[512,3584]{1,0:T(8,128)(2,1)} %bitcast.19), channel_id=1, source_target_pairs={{0,128},{128,0},{1,129},{129,1},{2,130},{130,2},{3,131},{131,3},{4... | collective-permute-start | bytes 11010056 | tf_op jit(solution)/shard_map/ppermute | solution.py:22
  0.5 43.2 %collective-permute-start.1 = (f32[1,512]{1,0:T(1,128)}, f32[1,512]{1,0:T(1,128)S(1)}, u32[]{:S(2)}, u32[]{:S(2)}) collective-permute-start(f32[1,512]{1,0:T(1,128)} %bias_own.3), channel_id=1, source_target_pairs={{0,128},{128,0},{1,129},{129,1},{2,130},{130,2},{3,131},{131,3},{4... | collective-permute-start | bytes 6152 | tf_op jit(solution)/shard_map/ppermute | solution.py:22
  0.5 43.2 %collective-permute-start = (f32[1,3584]{1,0:T(1,128)}, f32[1,3584]{1,0:T(1,128)S(1)}, u32[]{:S(2)}, u32[]{:S(2)}) collective-permute-start(f32[1,3584]{1,0:T(1,128)} %gain_own.3), channel_id=1, source_target_pairs={{0,128},{128,0},{1,129},{129,1},{2,130},{130,2},{3,131},{131,3},{4... | collective-permute-start | bytes 43016 | tf_op jit(solution)/shard_map/ppermute | solution.py:22
  2.5 41.2 %collective-permute-start.2 = (s32[1,4,2,1,4]{4,3,2,1,0:T(1,128)S(1)}, s32[1,4,2,1,4]{4,3,2,1,0:T(1,128)S(1)}, u32[]{:S(2)}, u32[]{:S(2)}) collective-permute-start(s32[1,4,2,1,4]{4,3,2,1,0:T(1,128)S(1)} %compare_select_fusion.list_own), channel_id=1, source_target_pairs={{0,128},{128,0},{1,129},{129,1},{2,130},{130,2},{3,131},{131,3},{4... | collective-permute-start | bytes 392 | tf_op jit(solution)/shard_map/ppermute | solution.py:22
  2.6 0.8 copy-start.2
  3.4 40.4 %copy-start = (f32[1,3584]{1,0:T(1,128)S(1)}, f32[1,3584]{1,0:T(1,128)}, u32[]{:S(2)}) copy-start(f32[1,3584]{1,0:T(1,128)} %gain_own.3) | copy-start | bytes 43012
  3.4 40.4 %copy-start.1 = (f32[1,512]{1,0:T(1,128)S(1)}, f32[1,512]{1,0:T(1,128)}, u32[]{:S(2)}) copy-start(f32[1,512]{1,0:T(1,128)} %bias_own.3) | copy-start | bytes 6148
  50.4 22.9 %all-to-all-start.4 = ((bf16[16,16,3584]{2,1,0:T(8,128)(2,1)}), bf16[16,16,3584]{2,1,0:T(8,128)(2,1)S(1)}, u32[]{:S(2)}, u32[]{:S(2)}) async-start(bf16[16,16,3584]{2,1,0:T(8,128)(2,1)} %get-tuple-element.24), calls=%async_computation.4 | async-start | bytes 3670016 | tf_op jit(solution)/shard_map/all_to_all | solution.py:26
